TPU v7x, 32 devices: a whole 2x2x4 slice. The times are simulated.
32 devices in a mesh: ctx: 8 (over z, y), fsdp: 4 (over x, core).
Axes of the slice: x: 2, y: 2, z: 4, core: 2. Of those that a mesh axis runs over, the one named last changes fastest.
Arguments:
- tokens: bfloat16 [4, 16, 128, 1024], P('fsdp', None, 'ctx'), may hold values from -6 to 6
- lengths: int32 [4, 3], P('fsdp'), may hold values from 512 to 1024, as said below
- packing: int32 [4, 3], P('fsdp'), may hold values from 0 to 2, each once within a row
- query_w: bfloat16 [1024, 1024], P('fsdp'), may hold values from -0.1875 to 0.1875
- query_b: float32 [1024], replicated, may hold values from -3 to 3
- key_w: bfloat16 [1024, 1024], P('fsdp'), may hold values from -0.1875 to 0.1875
- value_w: bfloat16 [1024, 1024], P('fsdp'), may hold values from -0.1875 to 0.1875
- value_b: float32 [1024], replicated, may hold values from -3 to 3
- output_w: bfloat16 [1024, 1024], P('fsdp'), may hold values from -3 to 3
- output_b: float32 [1024], replicated, may hold values from -3 to 3
- attn_gain: float32 [1024], replicated, may hold values from 0.5 to 1.5
- attn_shift: float32 [1024], replicated, may hold values from -2 to 2
- expand_w: bfloat16 [1024, 4096], P('fsdp'), may hold values from -0.1875 to 0.1875
- expand_b: float32 [4096], replicated, may hold values from -3 to 3
- reduce_w: bfloat16 [4096, 1024], P('fsdp'), may hold values from -0.09375 to 0.09375
- reduce_b: float32 [1024], replicated, may hold values from -3 to 3
- ffn_gain: float32 [1024], replicated, may hold values from 0.5 to 1.5
- ffn_shift: float32 [1024], replicated, may hold values from -2 to 2
- cotangent: bfloat16 [4, 16, 128, 1024], P('fsdp', None, 'ctx'), may hold values from -6 to 6
Outputs:
- layer_out: bfloat16 [4, 16, 128, 1024], P('fsdp', None, 'ctx')
- grad_tokens: float32 [4, 16, 128, 1024], P('fsdp', None, 'ctx')
- grad_query_w: float32 [1024, 1024], P('fsdp')
- grad_query_b: float32 [1024], replicated
- grad_key_w: float32 [1024, 1024], P('fsdp')
- grad_value_w: float32 [1024, 1024], P('fsdp')
- grad_value_b: float32 [1024], replicated
- grad_output_w: float32 [1024, 1024], P('fsdp')
- grad_output_b: float32 [1024], replicated
- grad_attn_gain: float32 [1024], replicated
- grad_attn_shift: float32 [1024], replicated
- grad_expand_w: float32 [1024, 4096], P('fsdp')
- grad_expand_b: float32 [4096], replicated
- grad_reduce_w: float32 [4096, 1024], P('fsdp')
- grad_reduce_b: float32 [1024], replicated
- grad_ffn_gain: float32 [1024], replicated
- grad_ffn_shift: float32 [1024], replicated
Inputs may be any that keep to these rules, and one draw needn't show every extreme that they name: Each row's 3 lengths sum to 2048. Each row of packing names every sequence once.
All inputs are finite; a program needn't handle non-finite values.
Results may differ from a plain program's by a relative error of at most 0.02.
Values may be sent and summed in bfloat16 or wider, within the bound.
A program may use at most 192 MiB of HBM per device.

v0:
```python
import jax
import jax.numpy as jnp
from jax import lax
from jax.sharding import PartitionSpec as P

H = 16
HD = 64


def from_behind(block, axis, distance):
    devices = range(lax.axis_size(axis))
    route = [((i - distance) % len(devices), i) for i in devices]
    return lax.ppermute(block, axis, route)


def dense(left, right):
    return jnp.dot(left, right, preferred_element_type=jnp.float32)


def dense_back(left, right):
    return lax.dot_general(
        left, right, (((1,), (1,)), ((), ())), preferred_element_type=jnp.float32
    )


def norm_fwd(hidden, gain, shift):
    mean_row = jnp.mean(hidden, axis=-1, keepdims=True)
    centred = hidden - mean_row
    variance = jnp.mean(centred * centred, axis=-1, keepdims=True)
    inv_std = lax.rsqrt(variance + 1e-05)
    x_hat = centred * inv_std
    return (x_hat * gain + shift, x_hat, inv_std)


def norm_back(incoming, x_hat, inv_std, gain):
    scaled = incoming * gain
    grad_in = inv_std * (
        scaled
        - jnp.mean(scaled, axis=-1, keepdims=True)
        - x_hat * jnp.mean(scaled * x_hat, axis=-1, keepdims=True)
    )
    return (grad_in, jnp.sum(incoming * x_hat, axis=0), jnp.sum(incoming, axis=0))


def gelu_slope(pre_act):
    return (
        0.5 * (1.0 + lax.erf(pre_act * 0.7071067811865476))
        + pre_act * jnp.exp(-0.5 * pre_act * pre_act) * 0.3989422804014327
    )


def online_update(running, query_heads, query_seg, key_rows, value_rows, key_seg):
    accum, run_max, run_sum = running
    rows_here = key_rows.shape[0]
    scores = 0.125 * jnp.einsum(
        "qhd,khd->hqk",
        query_heads,
        key_rows.reshape(rows_here, H, HD),
        preferred_element_type=jnp.float32,
    )
    same_seg = (query_seg[:, None] == key_seg[None, :])[None]
    masked = jnp.where(same_seg, scores, -1e30)
    new_max = jnp.maximum(run_max, jnp.max(masked, axis=-1))
    scale_old = jnp.exp(run_max - new_max)
    exp_scores = jnp.where(same_seg, jnp.exp(masked - new_max[:, :, None]), 0.0)
    run_sum = run_sum * scale_old + jnp.sum(exp_scores, axis=-1)
    update = jnp.einsum(
        "hqk,khd->qhd",
        exp_scores.astype(jnp.bfloat16),
        value_rows.reshape(rows_here, H, HD),
        preferred_element_type=jnp.float32,
    )
    accum = accum * scale_old.T[:, :, None] + update
    return (accum, new_max, run_sum)


def pair_grads(query_rows, grad_rows, log_sum, delta_row, query_seg, key_rows, value_rows, key_seg):
    q_heads = query_rows.reshape(-1, H, HD)
    g_heads = grad_rows.reshape(-1, H, HD)
    k_heads = key_rows.reshape(-1, H, HD)
    v_heads = value_rows.reshape(-1, H, HD)
    scores = 0.125 * jnp.einsum(
        "qhd,khd->hqk", q_heads, k_heads, preferred_element_type=jnp.float32
    )
    same_seg = (query_seg[:, None] == key_seg[None, :])[None]
    probs = jnp.where(
        same_seg, jnp.exp(jnp.where(same_seg, scores, -1e30) - log_sum[:, :, None]), 0.0
    )
    grad_prob = jnp.einsum("qhd,khd->hqk", g_heads, v_heads, preferred_element_type=jnp.float32)
    grad_score = (probs * (grad_prob - delta_row[:, :, None])).astype(jnp.bfloat16)
    grad_q = 0.125 * jnp.einsum(
        "hqk,khd->qhd", grad_score, k_heads, preferred_element_type=jnp.float32
    )
    grad_k = 0.125 * jnp.einsum(
        "hqk,qhd->khd", grad_score, q_heads, preferred_element_type=jnp.float32
    )
    grad_v = jnp.einsum(
        "hqk,qhd->khd", probs.astype(jnp.bfloat16), g_heads, preferred_element_type=jnp.float32
    )
    return (
        grad_q.reshape(query_rows.shape),
        grad_k.reshape(key_rows.shape),
        grad_v.reshape(key_rows.shape),
    )


def owner_rows(layer_in, layer_grad):
    return lax.psum_scatter(
        lax.dot_general(
            layer_in, layer_grad, (((0,), (0,)), ((), ())), preferred_element_type=jnp.float32
        ).astype(jnp.bfloat16),
        "fsdp",
        scatter_dimension=0,
        tiled=True,
    ).astype(jnp.float32)


def body(
    tokens,
    lengths,
    packing,
    query_w,
    query_b,
    key_w,
    value_w,
    value_b,
    output_w,
    output_b,
    attn_gain,
    attn_shift,
    expand_w,
    expand_b,
    reduce_w,
    reduce_b,
    ffn_gain,
    ffn_shift,
    cotangent,
):
    tok_shape = tokens.shape
    stripe = tok_shape[2]
    block_len = tok_shape[1] * tok_shape[2]
    model_width = tok_shape[3]
    n_ctx = lax.axis_size("ctx")
    ctx_index = lax.axis_index("ctx")
    seq_lens = lengths[0]
    slot_ids = packing[0]
    ordered = jnp.sum(
        jnp.where(
            slot_ids[:, None] == jnp.arange(seq_lens.shape[0], dtype=jnp.int32)[None, :],
            seq_lens[None, :],
            0,
        ),
        axis=1,
    )
    slot_ends = jnp.cumsum(ordered)
    gathered = jnp.arange(n_ctx * block_len, dtype=jnp.int32)
    owner_dev = gathered // block_len
    local_row = gathered % block_len
    position = local_row // stripe * (stripe * n_ctx) + owner_dev * stripe + local_row % stripe
    seg_all = jnp.sum((position[:, None] >= slot_ends[None, :]).astype(jnp.int32), axis=1)
    query_seg = lax.dynamic_slice_in_dim(seg_all, ctx_index * block_len, block_len)
    inputs = tokens.reshape(block_len, model_width)
    w_query, w_key, w_value, w_output, w_up, w_down = (
        lax.all_gather(query_w, "fsdp", axis=0, tiled=True),
        lax.all_gather(key_w, "fsdp", axis=0, tiled=True),
        lax.all_gather(value_w, "fsdp", axis=0, tiled=True),
        lax.all_gather(output_w, "fsdp", axis=0, tiled=True),
        lax.all_gather(expand_w, "fsdp", axis=0, tiled=True),
        lax.all_gather(reduce_w, "fsdp", axis=0, tiled=True),
    )
    queries = (dense(inputs, w_query) + query_b).astype(jnp.bfloat16)
    key_rows = dense(inputs, w_key).astype(jnp.bfloat16)
    values = (dense(inputs, w_value) + value_b).astype(jnp.bfloat16)
    query_heads = queries.reshape(block_len, H, HD)
    start_state = (
        jnp.zeros((block_len, H, HD), jnp.float32),
        jnp.full((H, block_len), -1e30, jnp.float32),
        jnp.zeros((H, block_len), jnp.float32),
    )
    key_piece = lax.all_gather(key_rows, "ctx", axis=0, tiled=True)
    value_piece = lax.all_gather(values, "ctx", axis=0, tiled=True)
    shards = key_piece.shape[0] // block_len

    def one_shard(index, inner):
        key_part = lax.dynamic_slice_in_dim(key_piece, index * block_len, block_len)
        value_part = lax.dynamic_slice_in_dim(value_piece, index * block_len, block_len)
        key_seg = lax.dynamic_slice_in_dim(seg_all, index * block_len, block_len)
        return online_update(inner, query_heads, query_seg, key_part, value_part, key_seg)

    accum, run_max, run_sum = lax.fori_loop(0, shards, one_shard, start_state)
    attended = (accum / run_sum.T[:, :, None]).reshape(block_len, model_width).astype(jnp.bfloat16)
    log_sum = run_max + jnp.log(run_sum)
    branch = dense(attended, w_output) + output_b
    normed, x_hat1, inv_std1 = norm_fwd(inputs.astype(jnp.float32) + branch, attn_gain, attn_shift)
    normed_low = normed.astype(jnp.bfloat16)
    pre_act = dense(normed_low, w_up) + expand_b
    hidden = jax.nn.gelu(pre_act, approximate=False).astype(jnp.bfloat16)
    ffn_out = dense(hidden, w_down) + reduce_b
    outputs, x_hat2, inv_std2 = norm_fwd(normed + ffn_out, ffn_gain, ffn_shift)
    layer_out = outputs.astype(jnp.bfloat16).reshape(tok_shape)
    upstream = cotangent.reshape(block_len, model_width).astype(jnp.float32)
    grad_mid2, grad_ffn_gain, grad_ffn_shift = norm_back(upstream, x_hat2, inv_std2, ffn_gain)
    grad_ffn = grad_mid2.astype(jnp.bfloat16)
    grad_reduce_b = jnp.sum(grad_ffn.astype(jnp.float32), axis=0)
    share_down = owner_rows(hidden, grad_ffn)
    grad_pre = (dense_back(grad_ffn, w_down) * gelu_slope(pre_act)).astype(jnp.bfloat16)
    grad_expand_b = jnp.sum(grad_pre.astype(jnp.float32), axis=0)
    share_up = owner_rows(normed_low, grad_pre)
    grad_normed = dense_back(grad_pre, w_up) + grad_mid2
    grad_mid1, grad_attn_gain, grad_attn_shift = norm_back(grad_normed, x_hat1, inv_std1, attn_gain)
    grad_branch = grad_mid1.astype(jnp.bfloat16)
    grad_output_b = jnp.sum(grad_branch.astype(jnp.float32), axis=0)
    share_out = owner_rows(attended, grad_branch)
    grad_att = dense_back(grad_branch, w_output).astype(jnp.bfloat16)
    delta_row = jnp.einsum(
        "qhd,qhd->hq",
        grad_att.astype(jnp.float32).reshape(block_len, H, HD),
        attended.astype(jnp.float32).reshape(block_len, H, HD),
    )
    zero_rows = jnp.zeros((block_len, model_width), jnp.float32)

    def key_step(step, state):
        visit_keys, visit_values, sum_k, sum_v, sum_q = state
        anchor = (ctx_index - step) % n_ctx
        key_seg = lax.dynamic_slice_in_dim(seg_all, anchor * block_len, block_len)
        part_q, part_k, part_v = pair_grads(
            queries, grad_att, log_sum, delta_row, query_seg, visit_keys, visit_values, key_seg
        )
        sum_q = sum_q + part_q
        visit_keys, visit_values = from_behind((visit_keys, visit_values), "ctx", 1)
        sum_k, sum_v = (
            from_behind((sum_k + part_k).astype(jnp.bfloat16), "ctx", 1).astype(jnp.float32),
            from_behind((sum_v + part_v).astype(jnp.bfloat16), "ctx", 1).astype(jnp.float32),
        )
        return (visit_keys, visit_values, sum_k, sum_v, sum_q)

    final = lax.fori_loop(0, n_ctx, key_step, (key_rows, values, zero_rows, zero_rows, zero_rows))
    sum_k, sum_v, sum_q = (final[2], final[3], final[4])
    grad_q = sum_q.astype(jnp.bfloat16)
    grad_k = sum_k.astype(jnp.bfloat16)
    grad_v = sum_v.astype(jnp.bfloat16)
    grad_query_b = jnp.sum(grad_q.astype(jnp.float32), axis=0)
    grad_value_b = jnp.sum(grad_v.astype(jnp.float32), axis=0)
    share_query = owner_rows(inputs, grad_q)
    share_key = owner_rows(inputs, grad_k)
    share_value = owner_rows(inputs, grad_v)
    grad_inputs = (
        dense_back(grad_q, w_query)
        + dense_back(grad_k, w_key)
        + dense_back(grad_v, w_value)
        + grad_mid1
    )
    share_query, share_key, share_value, share_out, share_up, share_down = lax.psum(
        (share_query, share_key, share_value, share_out, share_up, share_down), "ctx"
    )
    (
        grad_query_b,
        grad_value_b,
        grad_output_b,
        grad_attn_gain,
        grad_attn_shift,
        grad_expand_b,
        grad_reduce_b,
        grad_ffn_gain,
        grad_ffn_shift,
    ) = lax.psum(
        (
            grad_query_b,
            grad_value_b,
            grad_output_b,
            grad_attn_gain,
            grad_attn_shift,
            grad_expand_b,
            grad_reduce_b,
            grad_ffn_gain,
            grad_ffn_shift,
        ),
        ("ctx", "fsdp"),
    )
    return (
        layer_out,
        grad_inputs.reshape(tok_shape),
        share_query,
        grad_query_b,
        share_key,
        share_value,
        grad_value_b,
        share_out,
        grad_output_b,
        grad_attn_gain,
        grad_attn_shift,
        share_up,
        grad_expand_b,
        share_down,
        grad_reduce_b,
        grad_ffn_gain,
        grad_ffn_shift,
    )


def solution(mesh):
    return jax.shard_map(
        body,
        mesh=mesh,
        in_specs=(
            P("fsdp", None, "ctx", None),
            P("fsdp", None),
            P("fsdp", None),
            P("fsdp", None),
            P(),
            P("fsdp", None),
            P("fsdp", None),
            P(),
            P("fsdp", None),
            P(),
            P(),
            P(),
            P("fsdp", None),
            P(),
            P("fsdp", None),
            P(),
            P(),
            P(),
            P("fsdp", None, "ctx", None),
        ),
        out_specs=(
            P("fsdp", None, "ctx", None),
            P("fsdp", None, "ctx", None),
            P("fsdp", None),
            P(),
            P("fsdp", None),
            P("fsdp", None),
            P(),
            P("fsdp", None),
            P(),
            P(),
            P(),
            P("fsdp", None),
            P(),
            P("fsdp", None),
            P(),
            P(),
            P(),
        ),
        check_vma=False,
    )
```

profile of v0, /device:TPU:0, one launch (start us, length us, event | category | flops | bytes accessed | tf_op | source)
XLA Modules:
  0.0 1580.0 jit_solution(11764506689131481254)
XLA Ops:
  9.5 25.4 %all-gather.9.cloned.1.call-done = bf16[1024,1024]{1,0:T(8,128)(2,1)} async-done(((bf16[256,1024]{1,0:T(8,128)(2,1)}), bf16[1024,1024]{1,0:T(8,128)(2,1)}) %all-gather.9.cloned.1.call-update) | async-done | bytes 2097168 | tf_op jit(solution)/shard_map/all_gather | solution.py:165
  34.9 3.3 convolution_convert_fusion.4
  38.3 20.8 %all-gather.15.cloned.1.call-done = bf16[1024,1024]{1,0:T(8,128)(2,1)} async-done(((bf16[256,1024]{1,0:T(8,128)(2,1)}), bf16[1024,1024]{1,0:T(8,128)(2,1)}) %all-gather.15.cloned.1.call-update) | async-done | bytes 2097168 | tf_op jit(solution)/shard_map/all_gather | solution.py:166
  59.1 3.1 fusion.45
  67.9 15.4 all-gather.13.cloned.1.call-done
  85.8 73.5 %all-gather.11.cloned.1.call-done = bf16[2048,1024]{1,0:T(8,128)(2,1)} async-done(((bf16[256,1024]{1,0:T(8,128)(2,1)}), bf16[2048,1024]{1,0:T(8,128)(2,1)}) %all-gather.11.cloned.1.call-update) | async-done | bytes 4194320 | tf_op jit(solution)/shard_map/all_gather | solution.py:180
  159.3 74.2 %all-gather.17.cloned.1.call-done = bf16[2048,1024]{1,0:T(8,128)(2,1)} async-done(((bf16[256,1024]{1,0:T(8,128)(2,1)}), bf16[2048,1024]{1,0:T(8,128)(2,1)}) %all-gather.17.cloned.1.call-update) | async-done | bytes 4194320 | tf_op jit(solution)/shard_map/all_gather | solution.py:181
  233.5 103.5 %while.42 = (s32[]{:T(128)}, f32[256,16,64]{0,2,1:T(8,128)}, f32[16,256]{1,0:T(8,128)S(1)}, f32[16,256]{1,0:T(8,128)S(1)}, s32[256]{0:T(256)S(1)}, /*index=5*/s3...) while((s32[]{:T(128)}, f32[256,16,64]{0,2,1:T(8,128)}, ...), condition=%wide.region_6.7_spmd.clone, body=%wide.region_3.6_spmd.clone.sunk | while | flops 282943488 | bytes 20975804 | solution.py:190
  238.1 3.4 fusion.156
  241.7 4.3 fusion.155
  250.6 3.2 fusion.156
  254.1 4.6 fusion.155
  263.2 3.7 fusion.156
  267.2 5.8 fusion.155
  277.6 3.2 fusion.156
  281.0 4.7 fusion.155
  290.2 3.2 fusion.156
  293.6 4.6 fusion.155
  302.7 3.3 fusion.156
  306.2 4.6 fusion.155
  315.4 3.2 fusion.156
  318.8 4.6 fusion.155
  325.2 3.1 fusion.153
  328.3 3.9 fusion.156
  332.4 4.6 fusion.155
  341.4 15.8 fusion.29
  357.2 18.4 %all-gather.23.cloned.1.call-done = bf16[4096,1024]{1,0:T(8,128)(2,1)} async-done(((bf16[1024,1024]{1,0:T(8,128)(2,1)}), bf16[4096,1024]{1,0:T(8,128)(2,1)}) %all-gather.23.cloned.1.call-update) | async-done | bytes 8388624 | tf_op jit(solution)/shard_map/all_gather | solution.py:169
  375.6 6.6 fusion.88
  384.4 4.2 convert_reduce_fusion
  393.9 406.6 %while.43 = (s32[]{:T(128)}, bf16[256,1024]{0,1:T(8,128)(2,1)}, bf16[256,1024]{0,1:T(8,128)(2,1)}, f32[256,1024]{0,1:T(8,128)}, f32[256,1024]{0,1:T(8,128)}, /*i...) while((s32[]{:T(128)}, bf16[256,1024]{0,1:T(8,128)(2,1)}, ...), condition=%wide.region_16.17_spmd.clone, body=%wide.region_15.16_spmd.clone.sunk | while | flops 686882816 | bytes 68932264 | solution.py:237
  401.1 3.1 multiply_convert_fusion.2
  414.0 21.3 %collective-permute-done.2 = bf16[256,1024]{0,1:T(8,128)(2,1)} collective-permute-done((bf16[256,1024]{0,1:T(8,128)(2,1)}, bf16[256,1024]{0,1:T(8,128)(2,1)}, u32[]{:S(2)}, u32[]{:S(2)}) %collective-permute-start.2) | collective-permute-done | bytes 524320 | tf_op jit(solution)/shard_map/while/body/eval_jaxpr/ppermute | solution.py:13
  437.5 8.5 collective-permute-done.3
  453.3 3.1 multiply_convert_fusion.2
  466.2 23.3 %collective-permute-done.2 = bf16[256,1024]{0,1:T(8,128)(2,1)} collective-permute-done((bf16[256,1024]{0,1:T(8,128)(2,1)}, bf16[256,1024]{0,1:T(8,128)(2,1)}, u32[]{:S(2)}, u32[]{:S(2)}) %collective-permute-start.2) | collective-permute-done | bytes 524320 | tf_op jit(solution)/shard_map/while/body/eval_jaxpr/ppermute | solution.py:13
  491.5 7.6 collective-permute-done.3
  505.3 3.1 multiply_convert_fusion.2
  517.6 25.1 %collective-permute-done.2 = bf16[256,1024]{0,1:T(8,128)(2,1)} collective-permute-done((bf16[256,1024]{0,1:T(8,128)(2,1)}, bf16[256,1024]{0,1:T(8,128)(2,1)}, u32[]{:S(2)}, u32[]{:S(2)}) %collective-permute-start.2) | collective-permute-done | bytes 524320 | tf_op jit(solution)/shard_map/while/body/eval_jaxpr/ppermute | solution.py:13
  544.7 6.6 collective-permute-done.3
  557.5 3.1 multiply_convert_fusion.2
  568.0 26.8 %collective-permute-done.2 = bf16[256,1024]{0,1:T(8,128)(2,1)} collective-permute-done((bf16[256,1024]{0,1:T(8,128)(2,1)}, bf16[256,1024]{0,1:T(8,128)(2,1)}, u32[]{:S(2)}, u32[]{:S(2)}) %collective-permute-start.2) | collective-permute-done | bytes 524320 | tf_op jit(solution)/shard_map/while/body/eval_jaxpr/ppermute | solution.py:13
  596.9 5.7 collective-permute-done.3
  608.8 3.1 multiply_convert_fusion.2
  618.9 27.2 %collective-permute-done.2 = bf16[256,1024]{0,1:T(8,128)(2,1)} collective-permute-done((bf16[256,1024]{0,1:T(8,128)(2,1)}, bf16[256,1024]{0,1:T(8,128)(2,1)}, u32[]{:S(2)}, u32[]{:S(2)}) %collective-permute-start.2) | collective-permute-done | bytes 524320 | tf_op jit(solution)/shard_map/while/body/eval_jaxpr/ppermute | solution.py:13
  648.2 4.8 collective-permute-done.3
  659.1 3.1 multiply_convert_fusion.2
  669.2 27.2 %collective-permute-done.2 = bf16[256,1024]{0,1:T(8,128)(2,1)} collective-permute-done((bf16[256,1024]{0,1:T(8,128)(2,1)}, bf16[256,1024]{0,1:T(8,128)(2,1)}, u32[]{:S(2)}, u32[]{:S(2)}) %collective-permute-start.2) | collective-permute-done | bytes 524320 | tf_op jit(solution)/shard_map/while/body/eval_jaxpr/ppermute | solution.py:13
  698.5 3.8 collective-permute-done.3
  708.6 3.1 multiply_convert_fusion.2
  718.6 26.6 %collective-permute-done.2 = bf16[256,1024]{0,1:T(8,128)(2,1)} collective-permute-done((bf16[256,1024]{0,1:T(8,128)(2,1)}, bf16[256,1024]{0,1:T(8,128)(2,1)}, u32[]{:S(2)}, u32[]{:S(2)}) %collective-permute-start.2) | collective-permute-done | bytes 524320 | tf_op jit(solution)/shard_map/while/body/eval_jaxpr/ppermute | solution.py:13
  747.3 3.5 collective-permute-done.3
  757.1 3.1 multiply_convert_fusion.2
  767.1 25.7 %collective-permute-done.2 = bf16[256,1024]{0,1:T(8,128)(2,1)} collective-permute-done((bf16[256,1024]{0,1:T(8,128)(2,1)}, bf16[256,1024]{0,1:T(8,128)(2,1)}, u32[]{:S(2)}, u32[]{:S(2)}) %collective-permute-start.2) | collective-permute-done | bytes 524320 | tf_op jit(solution)/shard_map/while/body/eval_jaxpr/ppermute | solution.py:13
  794.9 3.5 collective-permute-done.3
  800.6 3.5 convert_bitcast_fusion.2
  808.5 3.7 convolution_convert_fusion.2
  812.2 7.3 convolution_convert_fusion.1
  820.8 7.2 convolution_convert_fusion
  829.5 38.5 %all-reduce = (f32[1024]{0:T(1024)}, f32[1024]{0:T(1024)}, f32[1024]{0:T(1024)}, f32[1024]{0:T(1024)}, f32[1024]{0:T(1024)}, /*index=5*/f32[4096]{0:T(1024)}, f32[1024]{0:T(1024)}, f32[1024]{0:T(1024)}, f32[1024]{0:T(1024)}) all-reduce(f32[1024]{0:T(1024)S(1)} %convert_reduce_fusion.5, ...), channel_id=1, replica_groups=mesh['ctx'=8,'fsdp'=4] {'ctx','fsdp'}, use_global_device_ids=true, to_apply=%region_20.21 | all-reduce | flops 12288 | bytes 98304 | tf_op jit(solution)/shard_map/psum | solution.py:266
  874.6 26.9 %reduce-scatter.11.cloned.1.call-done = bf16[256,1024]{0,1:T(8,128)(2,1)} async-done(((bf16[1024,1024]{0,1:T(8,128)(2,1)}), bf16[256,1024]{0,1:T(8,128)(2,1)}) %reduce-scatter.11.cloned.1.call-update) | async-done | bytes 524304 | tf_op jit(solution)/shard_map/reduce_scatter | solution.py:108
  901.5 34.0 %reduce-scatter.13.cloned.1.call-done = bf16[256,1024]{1,0:T(8,128)(2,1)} async-done(((bf16[1024,1024]{1,0:T(8,128)(2,1)}), bf16[256,1024]{1,0:T(8,128)(2,1)}) %reduce-scatter.13.cloned.1.call-update) | async-done | bytes 524304 | tf_op jit(solution)/shard_map/reduce_scatter | solution.py:108
  935.5 74.3 %reduce-scatter.15.cloned.1.call-done = bf16[256,4096]{1,0:T(8,128)(2,1)} async-done(((bf16[1024,4096]{1,0:T(8,128)(2,1)}), bf16[256,4096]{1,0:T(8,128)(2,1)}) %reduce-scatter.15.cloned.1.call-update) | async-done | bytes 2097168 | tf_op jit(solution)/shard_map/reduce_scatter | solution.py:108
  1009.8 74.4 %reduce-scatter.17.cloned.1.call-done = bf16[1024,1024]{1,0:T(8,128)(2,1)} async-done(((bf16[4096,1024]{1,0:T(8,128)(2,1)}), bf16[1024,1024]{1,0:T(8,128)(2,1)}) %reduce-scatter.17.cloned.1.call-update) | async-done | bytes 2097168 | tf_op jit(solution)/shard_map/reduce_scatter | solution.py:108
  1084.2 485.1 %all-reduce.3 = (f32[256,1024]{0,1:T(8,128)S(1)}, f32[256,1024]{0,1:T(8,128)S(1)}, f32[256,1024]{0,1:T(8,128)S(1)}, f32[256,1024]{1,0:T(8,128)}, f32[256,4096]{1,0:T(8,128)}, /*index=5*/f32[1024,1024]{1,0:T(8,128)}) all-reduce(bf16[256,1024]{0,1:T(8,128)(2,1)} %reduce-scatter.7.cloned.1.call-done, ...), channel_id=1, replica_groups=mesh['ctx'=8,'fsdp'=4] {'ctx'}, use_global_device_ids=true, to_apply=%region_18.19 | all-reduce | flops 3145728 | bytes 18874368 | tf_op jit(solution)/shard_map/psum | solution.py:253
  (471 shorter events, 208.2 us)
Async XLA Ops:
  7.2 51.9 %copy-start.11 = (bf16[1,16,16,1024]{3,2,1,0:T(8,128)(2,1)S(1)}, bf16[1,16,16,1024]{3,2,1,0:T(8,128)(2,1)}, u32[]{:S(2)}) copy-start(bf16[1,16,16,1024]{3,2,1,0:T(8,128)(2,1)} %param.23) | copy-start | bytes 1572868
  7.2 51.9 %copy-start.32 = (f32[1024]{0:T(1024)S(1)}, f32[1024]{0:T(1024)}, u32[]{:S(2)}) copy-start(f32[1024]{0:T(1024)} %param.30) | copy-start | bytes 12292
  7.2 27.7 %all-gather.9.cloned.1.call-start = ((), (), s32[]{:S(2)}) async-start(), calls=%async_computation.6 | async-start | bytes 2621440 | tf_op jit(solution)/shard_map/all_gather | solution.py:165
  7.9 51.2 %all-gather.15.cloned.1.call-start = ((), (), s32[]{:S(2)}) async-start(), calls=%async_computation.9 | async-start | bytes 2621440 | tf_op jit(solution)/shard_map/all_gather | solution.py:166
  8.7 74.6 %all-gather.13.cloned.1.call-start = ((), (), s32[]{:S(2)}) async-start(), calls=%async_computation.8 | async-start | bytes 2621440 | tf_op jit(solution)/shard_map/all_gather | solution.py:164
  9.4 149.9 %all-gather.11.cloned.1.call-start = ((), (), s32[]{:S(2)}) async-start(), calls=%async_computation.7 | async-start | bytes 4718592 | tf_op jit(solution)/shard_map/all_gather | solution.py:180
  38.3 195.3 %all-gather.17.cloned.1.call-start = ((), (), s32[]{:S(2)}) async-start(), calls=%async_computation.10 | async-start | bytes 4718592 | tf_op jit(solution)/shard_map/all_gather | solution.py:181
  62.2 276.2 %all-gather.19.cloned.1.call-start = ((), (), s32[]{:S(2)}) async-start(), calls=%async_computation.11 | async-start | bytes 2621440 | tf_op jit(solution)/shard_map/all_gather | solution.py:167
  62.8 278.6 %all-gather.21.cloned.1.call-start = ((), (), s32[]{:S(2)}) async-start(), calls=%async_computation.12 | async-start | bytes 10485760 | tf_op jit(solution)/shard_map/all_gather | solution.py:168
  63.6 312.0 %all-gather.23.cloned.1.call-start = ((), (), s32[]{:S(2)}) async-start(), calls=%async_computation.13 | async-start | bytes 10485760 | tf_op jit(solution)/shard_map/all_gather | solution.py:169
  64.3 810.3 %reduce-scatter.7.cloned.1.call-start = ((), (), s32[]{:S(2)}) async-start(), calls=%async_computation.14 | async-start | bytes 2621440 | tf_op jit(solution)/shard_map/reduce_scatter | solution.py:108
  233.5 104.9 %copy-start.28 = (f32[1024]{0:T(1024)S(1)}, f32[1024]{0:T(1024)}, u32[]{:S(2)}) copy-start(f32[1024]{0:T(1024)} %param.32) | copy-start | bytes 12292
  341.1 50.3 %copy-start.7 = (f32[256,1024]{1,0:T(8,128)}, f32[256,1024]{1,0:T(8,128)S(1)}, u32[]{:S(2)}) copy-start(f32[256,1024]{1,0:T(8,128)S(1)} %get-tuple-element.758) | copy-start | bytes 3145732
  341.4 34.2 %copy-start.34 = (f32[1024]{0:T(1024)S(1)}, f32[1024]{0:T(1024)}, u32[]{:S(2)}) copy-start(f32[1024]{0:T(1024)} %param.38) | copy-start | bytes 12292
  395.4 52.7 %collective-permute-start = (bf16[256,1024]{0,1:T(8,128)(2,1)S(1)}, bf16[256,1024]{0,1:T(8,128)(2,1)}, u32[]{:S(2)}, u32[]{:S(2)}) collective-permute-start(bf16[256,1024]{0,1:T(8,128)(2,1)S(1)} %copy.106), channel_id=1, source_target_pairs={{28,0},{0,4},{4,8},{8,12},{12,16},{16,20},{20,24},{24,28},{29,1},{... | collective-permute-start | bytes 1572872 | tf_op jit(solution)/shard_map/while/body/eval_jaxpr/ppermute | solution.py:13
  398.7 49.3 %collective-permute-start.1 = (bf16[256,1024]{0,1:T(8,128)(2,1)}, bf16[256,1024]{0,1:T(8,128)(2,1)}, u32[]{:S(2)}, u32[]{:S(2)}) collective-permute-start(bf16[256,1024]{0,1:T(8,128)(2,1)} %copy.107), channel_id=1, source_target_pairs={{28,0},{0,4},{4,8},{8,12},{12,16},{16,20},{20,24},{24,28},{29,1},{... | collective-permute-start | bytes 1572872 | tf_op jit(solution)/shard_map/while/body/eval_jaxpr/ppermute | solution.py:13
  406.4 29.0 %collective-permute-start.2 = (bf16[256,1024]{0,1:T(8,128)(2,1)}, bf16[256,1024]{0,1:T(8,128)(2,1)}, u32[]{:S(2)}, u32[]{:S(2)}) collective-permute-start(bf16[256,1024]{0,1:T(8,128)(2,1)} %fusion.169), channel_id=1, source_target_pairs={{28,0},{0,4},{4,8},{8,12},{12,16},{16,20},{20,24},{24,28},{29,1},{... | collective-permute-start | bytes 1572872 | tf_op jit(solution)/shard_map/while/body/eval_jaxpr/ppermute | solution.py:13
  411.1 34.8 %collective-permute-start.3 = (bf16[256,1024]{0,1:T(8,128)(2,1)}, bf16[256,1024]{0,1:T(8,128)(2,1)}, u32[]{:S(2)}, u32[]{:S(2)}) collective-permute-start(bf16[256,1024]{0,1:T(8,128)(2,1)} %fusion.171), channel_id=1, source_target_pairs={{28,0},{0,4},{4,8},{8,12},{12,16},{16,20},{20,24},{24,28},{29,1},{... | collective-permute-start | bytes 1572872 | tf_op jit(solution)/shard_map/while/body/eval_jaxpr/ppermute | solution.py:13
  413.3 34.7 %copy-start.22 = (bf16[256,1024]{0,1:T(8,128)(2,1)S(1)}, bf16[256,1024]{0,1:T(8,128)(2,1)}, u32[]{:S(2)}) copy-start(bf16[256,1024]{0,1:T(8,128)(2,1)} %copy-done.21) | copy-start | bytes 1572868 | tf_op jit(solution)/shard_map/while
  449.3 51.9 %collective-permute-start = (bf16[256,1024]{0,1:T(8,128)(2,1)S(1)}, bf16[256,1024]{0,1:T(8,128)(2,1)}, u32[]{:S(2)}, u32[]{:S(2)}) collective-permute-start(bf16[256,1024]{0,1:T(8,128)(2,1)S(1)} %copy.106), channel_id=1, source_target_pairs={{28,0},{0,4},{4,8},{8,12},{12,16},{16,20},{20,24},{24,28},{29,1},{... | collective-permute-start | bytes 1572872 | tf_op jit(solution)/shard_map/while/body/eval_jaxpr/ppermute | solution.py:13
  451.2 50.0 %collective-permute-start.1 = (bf16[256,1024]{0,1:T(8,128)(2,1)}, bf16[256,1024]{0,1:T(8,128)(2,1)}, u32[]{:S(2)}, u32[]{:S(2)}) collective-permute-start(bf16[256,1024]{0,1:T(8,128)(2,1)} %copy.107), channel_id=1, source_target_pairs={{28,0},{0,4},{4,8},{8,12},{12,16},{16,20},{20,24},{24,28},{29,1},{... | collective-permute-start | bytes 1572872 | tf_op jit(solution)/shard_map/while/body/eval_jaxpr/ppermute | solution.py:13
  458.6 30.9 %collective-permute-start.2 = (bf16[256,1024]{0,1:T(8,128)(2,1)}, bf16[256,1024]{0,1:T(8,128)(2,1)}, u32[]{:S(2)}, u32[]{:S(2)}) collective-permute-start(bf16[256,1024]{0,1:T(8,128)(2,1)} %fusion.169), channel_id=1, source_target_pairs={{28,0},{0,4},{4,8},{8,12},{12,16},{16,20},{20,24},{24,28},{29,1},{... | collective-permute-start | bytes 1572872 | tf_op jit(solution)/shard_map/while/body/eval_jaxpr/ppermute | solution.py:13
  462.4 36.7 %collective-permute-start.3 = (bf16[256,1024]{0,1:T(8,128)(2,1)}, bf16[256,1024]{0,1:T(8,128)(2,1)}, u32[]{:S(2)}, u32[]{:S(2)}) collective-permute-start(bf16[256,1024]{0,1:T(8,128)(2,1)} %fusion.171), channel_id=1, source_target_pairs={{28,0},{0,4},{4,8},{8,12},{12,16},{16,20},{20,24},{24,28},{29,1},{... | collective-permute-start | bytes 1572872 | tf_op jit(solution)/shard_map/while/body/eval_jaxpr/ppermute | solution.py:13
  465.5 35.7 %copy-start.22 = (bf16[256,1024]{0,1:T(8,128)(2,1)S(1)}, bf16[256,1024]{0,1:T(8,128)(2,1)}, u32[]{:S(2)}) copy-start(bf16[256,1024]{0,1:T(8,128)(2,1)} %copy-done.21) | copy-start | bytes 1572868 | tf_op jit(solution)/shard_map/while
  466.2 35.0 %copy-start.3 = (f32[256,1024]{0,1:T(8,128)}, f32[256,1024]{0,1:T(8,128)S(1)}, u32[]{:S(2)}) copy-start(f32[256,1024]{0,1:T(8,128)S(1)} %bitcast_add_fusion.4) | copy-start | bytes 3145732 | tf_op jit(solution)/shard_map/while
  502.5 50.9 %collective-permute-start = (bf16[256,1024]{0,1:T(8,128)(2,1)S(1)}, bf16[256,1024]{0,1:T(8,128)(2,1)}, u32[]{:S(2)}, u32[]{:S(2)}) collective-permute-start(bf16[256,1024]{0,1:T(8,128)(2,1)S(1)} %copy.106), channel_id=1, source_target_pairs={{28,0},{0,4},{4,8},{8,12},{12,16},{16,20},{20,24},{24,28},{29,1},{... | collective-permute-start | bytes 1572872 | tf_op jit(solution)/shard_map/while/body/eval_jaxpr/ppermute | solution.py:13
  504.3 49.1 %collective-permute-start.1 = (bf16[256,1024]{0,1:T(8,128)(2,1)}, bf16[256,1024]{0,1:T(8,128)(2,1)}, u32[]{:S(2)}, u32[]{:S(2)}) collective-permute-start(bf16[256,1024]{0,1:T(8,128)(2,1)} %copy.107), channel_id=1, source_target_pairs={{28,0},{0,4},{4,8},{8,12},{12,16},{16,20},{20,24},{24,28},{29,1},{... | collective-permute-start | bytes 1572872 | tf_op jit(solution)/shard_map/while/body/eval_jaxpr/ppermute | solution.py:13
  510.6 32.1 %collective-permute-start.2 = (bf16[256,1024]{0,1:T(8,128)(2,1)}, bf16[256,1024]{0,1:T(8,128)(2,1)}, u32[]{:S(2)}, u32[]{:S(2)}) collective-permute-start(bf16[256,1024]{0,1:T(8,128)(2,1)} %fusion.169), channel_id=1, source_target_pairs={{28,0},{0,4},{4,8},{8,12},{12,16},{16,20},{20,24},{24,28},{29,1},{... | collective-permute-start | bytes 1572872 | tf_op jit(solution)/shard_map/while/body/eval_jaxpr/ppermute | solution.py:13
  513.9 37.4 %collective-permute-start.3 = (bf16[256,1024]{0,1:T(8,128)(2,1)}, bf16[256,1024]{0,1:T(8,128)(2,1)}, u32[]{:S(2)}, u32[]{:S(2)}) collective-permute-start(bf16[256,1024]{0,1:T(8,128)(2,1)} %fusion.171), channel_id=1, source_target_pairs={{28,0},{0,4},{4,8},{8,12},{12,16},{16,20},{20,24},{24,28},{29,1},{... | collective-permute-start | bytes 1572872 | tf_op jit(solution)/shard_map/while/body/eval_jaxpr/ppermute | solution.py:13
  516.9 36.6 %copy-start.22 = (bf16[256,1024]{0,1:T(8,128)(2,1)S(1)}, bf16[256,1024]{0,1:T(8,128)(2,1)}, u32[]{:S(2)}) copy-start(bf16[256,1024]{0,1:T(8,128)(2,1)} %copy-done.21) | copy-start | bytes 1572868 | tf_op jit(solution)/shard_map/while
  517.5 35.9 %copy-start.3 = (f32[256,1024]{0,1:T(8,128)}, f32[256,1024]{0,1:T(8,128)S(1)}, u32[]{:S(2)}) copy-start(f32[256,1024]{0,1:T(8,128)S(1)} %bitcast_add_fusion.4) | copy-start | bytes 3145732 | tf_op jit(solution)/shard_map/while
  554.7 50.0 %collective-permute-start = (bf16[256,1024]{0,1:T(8,128)(2,1)S(1)}, bf16[256,1024]{0,1:T(8,128)(2,1)}, u32[]{:S(2)}, u32[]{:S(2)}) collective-permute-start(bf16[256,1024]{0,1:T(8,128)(2,1)S(1)} %copy.106), channel_id=1, source_target_pairs={{28,0},{0,4},{4,8},{8,12},{12,16},{16,20},{20,24},{24,28},{29,1},{... | collective-permute-start | bytes 1572872 | tf_op jit(solution)/shard_map/while/body/eval_jaxpr/ppermute | solution.py:13
  556.6 48.1 %collective-permute-start.1 = (bf16[256,1024]{0,1:T(8,128)(2,1)}, bf16[256,1024]{0,1:T(8,128)(2,1)}, u32[]{:S(2)}, u32[]{:S(2)}) collective-permute-start(bf16[256,1024]{0,1:T(8,128)(2,1)} %copy.107), channel_id=1, source_target_pairs={{28,0},{0,4},{4,8},{8,12},{12,16},{16,20},{20,24},{24,28},{29,1},{... | collective-permute-start | bytes 1572872 | tf_op jit(solution)/shard_map/while/body/eval_jaxpr/ppermute | solution.py:13
  562.8 32.0 %collective-permute-start.2 = (bf16[256,1024]{0,1:T(8,128)(2,1)}, bf16[256,1024]{0,1:T(8,128)(2,1)}, u32[]{:S(2)}, u32[]{:S(2)}) collective-permute-start(bf16[256,1024]{0,1:T(8,128)(2,1)} %fusion.169), channel_id=1, source_target_pairs={{28,0},{0,4},{4,8},{8,12},{12,16},{16,20},{20,24},{24,28},{29,1},{... | collective-permute-start | bytes 1572872 | tf_op jit(solution)/shard_map/while/body/eval_jaxpr/ppermute | solution.py:13
  566.1 36.5 %collective-permute-start.3 = (bf16[256,1024]{0,1:T(8,128)(2,1)}, bf16[256,1024]{0,1:T(8,128)(2,1)}, u32[]{:S(2)}, u32[]{:S(2)}) collective-permute-start(bf16[256,1024]{0,1:T(8,128)(2,1)} %fusion.171), channel_id=1, source_target_pairs={{28,0},{0,4},{4,8},{8,12},{12,16},{16,20},{20,24},{24,28},{29,1},{... | collective-permute-start | bytes 1572872 | tf_op jit(solution)/shard_map/while/body/eval_jaxpr/ppermute | solution.py:13
  567.3 37.4 %copy-start.22 = (bf16[256,1024]{0,1:T(8,128)(2,1)S(1)}, bf16[256,1024]{0,1:T(8,128)(2,1)}, u32[]{:S(2)}) copy-start(bf16[256,1024]{0,1:T(8,128)(2,1)} %copy-done.21) | copy-start | bytes 1572868 | tf_op jit(solution)/shard_map/while
  568.0 36.7 %copy-start.3 = (f32[256,1024]{0,1:T(8,128)}, f32[256,1024]{0,1:T(8,128)S(1)}, u32[]{:S(2)}) copy-start(f32[256,1024]{0,1:T(8,128)S(1)} %bitcast_add_fusion.4) | copy-start | bytes 3145732 | tf_op jit(solution)/shard_map/while
  605.9 49.1 %collective-permute-start = (bf16[256,1024]{0,1:T(8,128)(2,1)S(1)}, bf16[256,1024]{0,1:T(8,128)(2,1)}, u32[]{:S(2)}, u32[]{:S(2)}) collective-permute-start(bf16[256,1024]{0,1:T(8,128)(2,1)S(1)} %copy.106), channel_id=1, source_target_pairs={{28,0},{0,4},{4,8},{8,12},{12,16},{16,20},{20,24},{24,28},{29,1},{... | collective-permute-start | bytes 1572872 | tf_op jit(solution)/shard_map/while/body/eval_jaxpr/ppermute | solution.py:13
  607.8 47.2 %collective-permute-start.1 = (bf16[256,1024]{0,1:T(8,128)(2,1)}, bf16[256,1024]{0,1:T(8,128)(2,1)}, u32[]{:S(2)}, u32[]{:S(2)}) collective-permute-start(bf16[256,1024]{0,1:T(8,128)(2,1)} %copy.107), channel_id=1, source_target_pairs={{28,0},{0,4},{4,8},{8,12},{12,16},{16,20},{20,24},{24,28},{29,1},{... | collective-permute-start | bytes 1572872 | tf_op jit(solution)/shard_map/while/body/eval_jaxpr/ppermute | solution.py:13
  614.1 32.0 %collective-permute-start.2 = (bf16[256,1024]{0,1:T(8,128)(2,1)}, bf16[256,1024]{0,1:T(8,128)(2,1)}, u32[]{:S(2)}, u32[]{:S(2)}) collective-permute-start(bf16[256,1024]{0,1:T(8,128)(2,1)} %fusion.169), channel_id=1, source_target_pairs={{28,0},{0,4},{4,8},{8,12},{12,16},{16,20},{20,24},{24,28},{29,1},{... | collective-permute-start | bytes 1572872 | tf_op jit(solution)/shard_map/while/body/eval_jaxpr/ppermute | solution.py:13
  617.4 35.5 %collective-permute-start.3 = (bf16[256,1024]{0,1:T(8,128)(2,1)}, bf16[256,1024]{0,1:T(8,128)(2,1)}, u32[]{:S(2)}, u32[]{:S(2)}) collective-permute-start(bf16[256,1024]{0,1:T(8,128)(2,1)} %fusion.171), channel_id=1, source_target_pairs={{28,0},{0,4},{4,8},{8,12},{12,16},{16,20},{20,24},{24,28},{29,1},{... | collective-permute-start | bytes 1572872 | tf_op jit(solution)/shard_map/while/body/eval_jaxpr/ppermute | solution.py:13
  618.2 36.9 %copy-start.22 = (bf16[256,1024]{0,1:T(8,128)(2,1)S(1)}, bf16[256,1024]{0,1:T(8,128)(2,1)}, u32[]{:S(2)}) copy-start(bf16[256,1024]{0,1:T(8,128)(2,1)} %copy-done.21) | copy-start | bytes 1572868 | tf_op jit(solution)/shard_map/while
  618.8 36.2 %copy-start.3 = (f32[256,1024]{0,1:T(8,128)}, f32[256,1024]{0,1:T(8,128)S(1)}, u32[]{:S(2)}) copy-start(f32[256,1024]{0,1:T(8,128)S(1)} %bitcast_add_fusion.4) | copy-start | bytes 3145732 | tf_op jit(solution)/shard_map/while
  656.3 48.1 %collective-permute-start = (bf16[256,1024]{0,1:T(8,128)(2,1)S(1)}, bf16[256,1024]{0,1:T(8,128)(2,1)}, u32[]{:S(2)}, u32[]{:S(2)}) collective-permute-start(bf16[256,1024]{0,1:T(8,128)(2,1)S(1)} %copy.106), channel_id=1, source_target_pairs={{28,0},{0,4},{4,8},{8,12},{12,16},{16,20},{20,24},{24,28},{29,1},{... | collective-permute-start | bytes 1572872 | tf_op jit(solution)/shard_map/while/body/eval_jaxpr/ppermute | solution.py:13
  658.2 46.3 %collective-permute-start.1 = (bf16[256,1024]{0,1:T(8,128)(2,1)}, bf16[256,1024]{0,1:T(8,128)(2,1)}, u32[]{:S(2)}, u32[]{:S(2)}) collective-permute-start(bf16[256,1024]{0,1:T(8,128)(2,1)} %copy.107), channel_id=1, source_target_pairs={{28,0},{0,4},{4,8},{8,12},{12,16},{16,20},{20,24},{24,28},{29,1},{... | collective-permute-start | bytes 1572872 | tf_op jit(solution)/shard_map/while/body/eval_jaxpr/ppermute | solution.py:13
  664.4 32.0 %collective-permute-start.2 = (bf16[256,1024]{0,1:T(8,128)(2,1)}, bf16[256,1024]{0,1:T(8,128)(2,1)}, u32[]{:S(2)}, u32[]{:S(2)}) collective-permute-start(bf16[256,1024]{0,1:T(8,128)(2,1)} %fusion.169), channel_id=1, source_target_pairs={{28,0},{0,4},{4,8},{8,12},{12,16},{16,20},{20,24},{24,28},{29,1},{... | collective-permute-start | bytes 1572872 | tf_op jit(solution)/shard_map/while/body/eval_jaxpr/ppermute | solution.py:13
  667.7 34.6 %collective-permute-start.3 = (bf16[256,1024]{0,1:T(8,128)(2,1)}, bf16[256,1024]{0,1:T(8,128)(2,1)}, u32[]{:S(2)}, u32[]{:S(2)}) collective-permute-start(bf16[256,1024]{0,1:T(8,128)(2,1)} %fusion.171), channel_id=1, source_target_pairs={{28,0},{0,4},{4,8},{8,12},{12,16},{16,20},{20,24},{24,28},{29,1},{... | collective-permute-start | bytes 1572872 | tf_op jit(solution)/shard_map/while/body/eval_jaxpr/ppermute | solution.py:13
  668.5 35.9 %copy-start.22 = (bf16[256,1024]{0,1:T(8,128)(2,1)S(1)}, bf16[256,1024]{0,1:T(8,128)(2,1)}, u32[]{:S(2)}) copy-start(bf16[256,1024]{0,1:T(8,128)(2,1)} %copy-done.21) | copy-start | bytes 1572868 | tf_op jit(solution)/shard_map/while
  669.2 35.3 %copy-start.3 = (f32[256,1024]{0,1:T(8,128)}, f32[256,1024]{0,1:T(8,128)S(1)}, u32[]{:S(2)}) copy-start(f32[256,1024]{0,1:T(8,128)S(1)} %bitcast_add_fusion.4) | copy-start | bytes 3145732 | tf_op jit(solution)/shard_map/while
  705.7 47.2 %collective-permute-start = (bf16[256,1024]{0,1:T(8,128)(2,1)S(1)}, bf16[256,1024]{0,1:T(8,128)(2,1)}, u32[]{:S(2)}, u32[]{:S(2)}) collective-permute-start(bf16[256,1024]{0,1:T(8,128)(2,1)S(1)} %copy.106), channel_id=1, source_target_pairs={{28,0},{0,4},{4,8},{8,12},{12,16},{16,20},{20,24},{24,28},{29,1},{... | collective-permute-start | bytes 1572872 | tf_op jit(solution)/shard_map/while/body/eval_jaxpr/ppermute | solution.py:13
  707.6 45.4 %collective-permute-start.1 = (bf16[256,1024]{0,1:T(8,128)(2,1)}, bf16[256,1024]{0,1:T(8,128)(2,1)}, u32[]{:S(2)}, u32[]{:S(2)}) collective-permute-start(bf16[256,1024]{0,1:T(8,128)(2,1)} %copy.107), channel_id=1, source_target_pairs={{28,0},{0,4},{4,8},{8,12},{12,16},{16,20},{20,24},{24,28},{29,1},{... | collective-permute-start | bytes 1572872 | tf_op jit(solution)/shard_map/while/body/eval_jaxpr/ppermute | solution.py:13
  713.8 31.4 %collective-permute-start.2 = (bf16[256,1024]{0,1:T(8,128)(2,1)}, bf16[256,1024]{0,1:T(8,128)(2,1)}, u32[]{:S(2)}, u32[]{:S(2)}) collective-permute-start(bf16[256,1024]{0,1:T(8,128)(2,1)} %fusion.169), channel_id=1, source_target_pairs={{28,0},{0,4},{4,8},{8,12},{12,16},{16,20},{20,24},{24,28},{29,1},{... | collective-permute-start | bytes 1572872 | tf_op jit(solution)/shard_map/while/body/eval_jaxpr/ppermute | solution.py:13
  717.2 33.7 %collective-permute-start.3 = (bf16[256,1024]{0,1:T(8,128)(2,1)}, bf16[256,1024]{0,1:T(8,128)(2,1)}, u32[]{:S(2)}, u32[]{:S(2)}) collective-permute-start(bf16[256,1024]{0,1:T(8,128)(2,1)} %fusion.171), channel_id=1, source_target_pairs={{28,0},{0,4},{4,8},{8,12},{12,16},{16,20},{20,24},{24,28},{29,1},{... | collective-permute-start | bytes 1572872 | tf_op jit(solution)/shard_map/while/body/eval_jaxpr/ppermute | solution.py:13
  717.9 35.0 %copy-start.22 = (bf16[256,1024]{0,1:T(8,128)(2,1)S(1)}, bf16[256,1024]{0,1:T(8,128)(2,1)}, u32[]{:S(2)}) copy-start(bf16[256,1024]{0,1:T(8,128)(2,1)} %copy-done.21) | copy-start | bytes 1572868 | tf_op jit(solution)/shard_map/while
  718.6 34.3 %copy-start.3 = (f32[256,1024]{0,1:T(8,128)}, f32[256,1024]{0,1:T(8,128)S(1)}, u32[]{:S(2)}) copy-start(f32[256,1024]{0,1:T(8,128)S(1)} %bitcast_add_fusion.4) | copy-start | bytes 3145732 | tf_op jit(solution)/shard_map/while
  754.2 46.3 %collective-permute-start = (bf16[256,1024]{0,1:T(8,128)(2,1)S(1)}, bf16[256,1024]{0,1:T(8,128)(2,1)}, u32[]{:S(2)}, u32[]{:S(2)}) collective-permute-start(bf16[256,1024]{0,1:T(8,128)(2,1)S(1)} %copy.106), channel_id=1, source_target_pairs={{28,0},{0,4},{4,8},{8,12},{12,16},{16,20},{20,24},{24,28},{29,1},{... | collective-permute-start | bytes 1572872 | tf_op jit(solution)/shard_map/while/body/eval_jaxpr/ppermute | solution.py:13
  756.1 44.4 %collective-permute-start.1 = (bf16[256,1024]{0,1:T(8,128)(2,1)}, bf16[256,1024]{0,1:T(8,128)(2,1)}, u32[]{:S(2)}, u32[]{:S(2)}) collective-permute-start(bf16[256,1024]{0,1:T(8,128)(2,1)} %copy.107), channel_id=1, source_target_pairs={{28,0},{0,4},{4,8},{8,12},{12,16},{16,20},{20,24},{24,28},{29,1},{... | collective-permute-start | bytes 1572872 | tf_op jit(solution)/shard_map/while/body/eval_jaxpr/ppermute | solution.py:13
  762.3 30.5 %collective-permute-start.2 = (bf16[256,1024]{0,1:T(8,128)(2,1)}, bf16[256,1024]{0,1:T(8,128)(2,1)}, u32[]{:S(2)}, u32[]{:S(2)}) collective-permute-start(bf16[256,1024]{0,1:T(8,128)(2,1)} %fusion.169), channel_id=1, source_target_pairs={{28,0},{0,4},{4,8},{8,12},{12,16},{16,20},{20,24},{24,28},{29,1},{... | collective-permute-start | bytes 1572872 | tf_op jit(solution)/shard_map/while/body/eval_jaxpr/ppermute | solution.py:13
  765.7 32.8 %collective-permute-start.3 = (bf16[256,1024]{0,1:T(8,128)(2,1)}, bf16[256,1024]{0,1:T(8,128)(2,1)}, u32[]{:S(2)}, u32[]{:S(2)}) collective-permute-start(bf16[256,1024]{0,1:T(8,128)(2,1)} %fusion.171), channel_id=1, source_target_pairs={{28,0},{0,4},{4,8},{8,12},{12,16},{16,20},{20,24},{24,28},{29,1},{... | collective-permute-start | bytes 1572872 | tf_op jit(solution)/shard_map/while/body/eval_jaxpr/ppermute | solution.py:13
  804.1 70.5 %reduce-scatter.9.cloned.1.call-start = ((), (), s32[]{:S(2)}) async-start(), calls=%async_computation.15 | async-start | bytes 2621440 | tf_op jit(solution)/shard_map/reduce_scatter | solution.py:108
  806.3 95.2 %reduce-scatter.11.cloned.1.call-start = ((), (), s32[]{:S(2)}) async-start(), calls=%async_computation.16 | async-start | bytes 2621440 | tf_op jit(solution)/shard_map/reduce_scatter | solution.py:108
  808.4 127.1 %reduce-scatter.13.cloned.1.call-start = ((), (), s32[]{:S(2)}) async-start(), calls=%async_computation.17 | async-start | bytes 2621440 | tf_op jit(solution)/shard_map/reduce_scatter | solution.py:108
  812.2 197.6 %reduce-scatter.15.cloned.1.call-start = ((), (), s32[]{:S(2)}) async-start(), calls=%async_computation.18 | async-start | bytes 10485760 | tf_op jit(solution)/shard_map/reduce_scatter | solution.py:108
  819.6 264.6 %reduce-scatter.17.cloned.1.call-start = ((), (), s32[]{:S(2)}) async-start(), calls=%async_computation.19 | async-start | bytes 10485760 | tf_op jit(solution)/shard_map/reduce_scatter | solution.py:108
  (66 other events, 447.8 us)
Sparse Core Ops, SparseCore 0:
  9.6 25.2 all-gather.8
  36.5 22.5 all-gather.14
  60.7 22.5 all-gather.12
  85.8 73.3 all-gather.10
  161.8 71.6 all-gather.16
  234.9 20.8 all-gather.18
  257.4 58.2 all-gather.20
  317.3 58.2 all-gather.22
  804.2 28.1 reduce-scatter.6
  834.9 32.4 reduce-scatter.8
  870.0 31.4 reduce-scatter.10
  904.0 31.4 reduce-scatter.12
  938.1 71.6 reduce-scatter.14
  1012.4 71.6 reduce-scatter.16
where the time goes:
time: 1590 us; the launch traced here: 1580 us
  waiting for transfers between devices  689 us (43%)
  blocking collectives  524 us (33%)
  matrix products  194 us (12%)
  other arithmetic  85.1 us (5%)
  local copies, waits for them, and re-layouts  59 us (4%)
    psum x1, blocking collectives, body(): lax.psum((share_query, share_key, share_value, share_out, share_up, share...  485 us
    ppermute x32, waiting for transfers between devices, from_behind(): return lax.ppermute(block, axis, route)  247 us
    reduce_scatter x6, waiting for transfers between devices, owner_rows(): lax.psum_scatter(lax.dot_general(layer_in, layer_grad, (((0,), (0,)), (()...  210 us
    all_gather x1, waiting for transfers between devices, body(): value_piece = lax.all_gather(values, 'ctx', axis=0, tiled=True)  74.2 us
    all_gather x1, waiting for transfers between devices, body(): key_piece = lax.all_gather(key_rows, 'ctx', axis=0, tiled=True)  73.5 us
    psum x1, blocking collectives, body(): lax.psum((grad_query_b, grad_value_b, grad_output_b, grad_attn_gain, grad...  38.5 us
    dot_general x8, matrix products, online_update(): jnp.einsum('hqk,khd->qhd', exp_scores.astype(jnp.bfloat16), value_rows.re...  37.9 us
    while x120, local copies, waits for them, and re-layouts  34.6 us
  transfers between devices with their start and end apart: 46, of which 26 were waited for; matrix products, arithmetic and copies ran while one was open for 18% of the time, Pallas kernels for 0%

commit v1 on v0

--- a/solution.py
+++ b/solution.py
@@ -264,18 +264,21 @@
         grad_ffn_gain,
         grad_ffn_shift,
     ) = lax.psum(
-        (
-            grad_query_b,
-            grad_value_b,
-            grad_output_b,
-            grad_attn_gain,
-            grad_attn_shift,
-            grad_expand_b,
-            grad_reduce_b,
-            grad_ffn_gain,
-            grad_ffn_shift,
+        lax.psum(
+            (
+                grad_query_b,
+                grad_value_b,
+                grad_output_b,
+                grad_attn_gain,
+                grad_attn_shift,
+                grad_expand_b,
+                grad_reduce_b,
+                grad_ffn_gain,
+                grad_ffn_shift,
+            ),
+            "fsdp",
         ),
-        ("ctx", "fsdp"),
+        "ctx",
     )
     return (
         layer_out,

time: 1590 us -> 1590 us (level)
  blocking collectives: 524 us -> 498 us
  waiting for transfers between devices: 689 us -> 713 us
  matrix products: 194 us -> 216 us
  other arithmetic: 85.1 us -> 66.6 us
    psum x1, blocking collectives: 38.5 us -> 10.6 us  [body(): lax.psum((grad_query_b, grad_value_b, grad_output_b, grad_attn_gain, grad...]
    reduce_scatter x6, waiting for transfers between devices: 210 us -> 236 us  [owner_rows(): lax.psum_scatter(lax.dot_general(layer_in, layer_grad, (((0,), (0,)), (()...]
    ppermute x32, waiting for transfers between devices: 247 us -> 228 us  [from_behind(): return lax.ppermute(block, axis, route)]
    reduce_sum x8, other arithmetic: 27.1 us -> 8 us  [online_update(): run_sum = run_sum * scale_old + jnp.sum(exp_scores, axis=-1)]
    all_gather x1, waiting for transfers between devices: 18.4 us -> 36.1 us  [body(): lax.all_gather(reduce_w, 'fsdp', axis=0, tiled=True)]
    dot_general x8, matrix products: 6.03 us -> 22.1 us  [pair_grads(): jnp.einsum('qhd,khd->hqk', q_heads, k_heads, preferred_element_type=jnp.f...]
    while x120 -> x152, local copies, waits for them, and re-layouts: 34.6 us -> 34.2 us
  transfers between devices with their start and end apart: 46 -> 46, of which waited for: 26 -> 27; matrix products, arithmetic and copies ran while one was open for 18% -> 19% of each run, Pallas kernels for 0% -> 0%
where the time goes in v1:
time: 1590 us; the launch traced here: 1580 us
  waiting for transfers between devices  713 us (45%)
  blocking collectives  498 us (31%)
  matrix products  216 us (14%)
  other arithmetic  66.6 us (4%)
  local copies, waits for them, and re-layouts  59.1 us (4%)
    psum x1, blocking collectives, body(): lax.psum((share_query, share_key, share_value, share_out, share_up, share...  488 us
    reduce_scatter x6, waiting for transfers between devices, owner_rows(): lax.psum_scatter(lax.dot_general(layer_in, layer_grad, (((0,), (0,)), (()...  236 us
    ppermute x32, waiting for transfers between devices, from_behind(): return lax.ppermute(block, axis, route)  228 us
    all_gather x1, waiting for transfers between devices, body(): value_piece = lax.all_gather(values, 'ctx', axis=0, tiled=True)  74.2 us
    all_gather x1, waiting for transfers between devices, body(): key_piece = lax.all_gather(key_rows, 'ctx', axis=0, tiled=True)  73.5 us
    dot_general x8, matrix products, online_update(): jnp.einsum('hqk,khd->qhd', exp_scores.astype(jnp.bfloat16), value_rows.re...  38.4 us
    all_gather x1, waiting for transfers between devices, body(): lax.all_gather(reduce_w, 'fsdp', axis=0, tiled=True)  36.1 us
    dot_general x6, matrix products, dense(): return jnp.dot(left, right, preferred_element_type=jnp.float32)  34.3 us
  transfers between devices with their start and end apart: 46, of which 27 were waited for; matrix products, arithmetic and copies ran while one was open for 19% of the time, Pallas kernels for 0%

profile of v1, /device:TPU:0, one launch (start us, length us, event | category | flops | bytes accessed | tf_op | source)
XLA Modules:
  0.0 1581.6 jit_solution(13568383973849568858)
XLA Ops:
  9.5 25.4 %all-gather.9.cloned.1.call-done = bf16[1024,1024]{1,0:T(8,128)(2,1)} async-done(((bf16[256,1024]{1,0:T(8,128)(2,1)}), bf16[1024,1024]{1,0:T(8,128)(2,1)}) %all-gather.9.cloned.1.call-update) | async-done | bytes 2097168 | tf_op jit(solution)/shard_map/all_gather | solution.py:165
  34.9 3.3 convolution_convert_fusion.4
  38.3 20.8 %all-gather.15.cloned.1.call-done = bf16[1024,1024]{1,0:T(8,128)(2,1)} async-done(((bf16[256,1024]{1,0:T(8,128)(2,1)}), bf16[1024,1024]{1,0:T(8,128)(2,1)}) %all-gather.15.cloned.1.call-update) | async-done | bytes 2097168 | tf_op jit(solution)/shard_map/all_gather | solution.py:166
  59.1 3.1 fusion.45
  67.9 15.4 all-gather.13.cloned.1.call-done
  85.8 73.5 %all-gather.11.cloned.1.call-done = bf16[2048,1024]{1,0:T(8,128)(2,1)} async-done(((bf16[256,1024]{1,0:T(8,128)(2,1)}), bf16[2048,1024]{1,0:T(8,128)(2,1)}) %all-gather.11.cloned.1.call-update) | async-done | bytes 4194320 | tf_op jit(solution)/shard_map/all_gather | solution.py:180
  159.3 74.2 %all-gather.17.cloned.1.call-done = bf16[2048,1024]{1,0:T(8,128)(2,1)} async-done(((bf16[256,1024]{1,0:T(8,128)(2,1)}), bf16[2048,1024]{1,0:T(8,128)(2,1)}) %all-gather.17.cloned.1.call-update) | async-done | bytes 4194320 | tf_op jit(solution)/shard_map/all_gather | solution.py:181
  233.5 85.1 %while.42 = (s32[]{:T(128)}, f32[256,16,64]{0,2,1:T(8,128)}, f32[16,256]{1,0:T(8,128)S(1)}, f32[16,256]{1,0:T(8,128)S(1)}, s32[256]{0:T(256)S(1)}, /*index=5*/s3...) while((s32[]{:T(128)}, f32[256,16,64]{0,2,1:T(8,128)}, ...), condition=%wide.region_6.7_spmd.clone, body=%wide.region_3.6_spmd.clone.sunk | while | flops 282943488 | bytes 37753056 | solution.py:190
  235.4 2.8 fusion.153
  238.3 4.7 fusion.155
  246.0 2.8 fusion.153
  248.8 4.8 fusion.155
  256.6 2.8 fusion.153
  259.5 4.8 fusion.155
  267.4 2.8 fusion.153
  270.2 4.8 fusion.155
  278.0 2.8 fusion.153
  280.8 4.8 fusion.155
  288.6 2.8 fusion.153
  291.5 4.8 fusion.155
  299.3 2.8 fusion.153
  302.1 4.8 fusion.155
  309.9 2.8 fusion.153
  312.8 4.8 fusion.155
  323.0 16.4 %fusion.29 = (bf16[256,4096]{1,0:T(8,128)(2,1)}, f32[256,4096]{1,0:T(8,128)}) fusion(f32[4096]{0:T(1024)S(1)} %copy-done.33, bf16[1024,4096]{1,0:T(8,128)(2,1)} %all-gather.21.cloned.1.call-done, f32[256,1024]{1,0:T(8,128)S(1)} %get-tuple-element.767, f32[1024]{0:T(1024)S(1)} %copy-done.28, f32[1024]{0:T(1024)S(1)} %copy-done.27, ...), kind=kOutput, calls=%fused_computation.46 | convolution fusion | flops 2218000384 | bytes 15755264 | tf_op jit(solution)/shard_map/dot_general | solution.py:17
  339.5 36.1 %all-gather.23.cloned.1.call-done = bf16[4096,1024]{1,0:T(8,128)(2,1)} async-done(((bf16[1024,1024]{1,0:T(8,128)(2,1)}), bf16[4096,1024]{1,0:T(8,128)(2,1)}) %all-gather.23.cloned.1.call-update) | async-done | bytes 8388624 | tf_op jit(solution)/shard_map/all_gather | solution.py:169
  375.6 6.6 fusion.88
  384.4 4.2 convert_reduce_fusion
  393.9 406.8 %while.43 = (s32[]{:T(128)}, bf16[256,1024]{0,1:T(8,128)(2,1)}, bf16[256,1024]{0,1:T(8,128)(2,1)}, f32[256,1024]{0,1:T(8,128)}, f32[256,1024]{0,1:T(8,128)}, /*i...) while((s32[]{:T(128)}, bf16[256,1024]{0,1:T(8,128)(2,1)}, ...), condition=%wide.region_16.17_spmd.clone, body=%wide.region_15.16_spmd.clone.sunk | while | flops 686882816 | bytes 85709512 | solution.py:237
  403.2 3.8 multiply_convert_fusion.2
  416.1 19.3 %collective-permute-done.2 = bf16[256,1024]{0,1:T(8,128)(2,1)} collective-permute-done((bf16[256,1024]{0,1:T(8,128)(2,1)}, bf16[256,1024]{0,1:T(8,128)(2,1)}, u32[]{:S(2)}, u32[]{:S(2)}) %collective-permute-start.2) | collective-permute-done | bytes 524320 | tf_op jit(solution)/shard_map/while/body/eval_jaxpr/ppermute | solution.py:13
  437.5 8.5 collective-permute-done.3
  455.3 3.8 multiply_convert_fusion.2
  468.2 21.2 %collective-permute-done.2 = bf16[256,1024]{0,1:T(8,128)(2,1)} collective-permute-done((bf16[256,1024]{0,1:T(8,128)(2,1)}, bf16[256,1024]{0,1:T(8,128)(2,1)}, u32[]{:S(2)}, u32[]{:S(2)}) %collective-permute-start.2) | collective-permute-done | bytes 524320 | tf_op jit(solution)/shard_map/while/body/eval_jaxpr/ppermute | solution.py:13
  491.5 7.6 collective-permute-done.3
  507.3 3.8 multiply_convert_fusion.2
  519.6 23.0 %collective-permute-done.2 = bf16[256,1024]{0,1:T(8,128)(2,1)} collective-permute-done((bf16[256,1024]{0,1:T(8,128)(2,1)}, bf16[256,1024]{0,1:T(8,128)(2,1)}, u32[]{:S(2)}, u32[]{:S(2)}) %collective-permute-start.2) | collective-permute-done | bytes 524320 | tf_op jit(solution)/shard_map/while/body/eval_jaxpr/ppermute | solution.py:13
  544.7 6.6 collective-permute-done.3
  559.5 3.8 multiply_convert_fusion.2
  570.4 24.4 %collective-permute-done.2 = bf16[256,1024]{0,1:T(8,128)(2,1)} collective-permute-done((bf16[256,1024]{0,1:T(8,128)(2,1)}, bf16[256,1024]{0,1:T(8,128)(2,1)}, u32[]{:S(2)}, u32[]{:S(2)}) %collective-permute-start.2) | collective-permute-done | bytes 524320 | tf_op jit(solution)/shard_map/while/body/eval_jaxpr/ppermute | solution.py:13
  596.9 5.7 collective-permute-done.3
  610.8 3.8 multiply_convert_fusion.2
  621.7 24.4 %collective-permute-done.2 = bf16[256,1024]{0,1:T(8,128)(2,1)} collective-permute-done((bf16[256,1024]{0,1:T(8,128)(2,1)}, bf16[256,1024]{0,1:T(8,128)(2,1)}, u32[]{:S(2)}, u32[]{:S(2)}) %collective-permute-start.2) | collective-permute-done | bytes 524320 | tf_op jit(solution)/shard_map/while/body/eval_jaxpr/ppermute | solution.py:13
  648.2 4.8 collective-permute-done.3
  661.2 3.8 multiply_convert_fusion.2
  672.1 24.4 %collective-permute-done.2 = bf16[256,1024]{0,1:T(8,128)(2,1)} collective-permute-done((bf16[256,1024]{0,1:T(8,128)(2,1)}, bf16[256,1024]{0,1:T(8,128)(2,1)}, u32[]{:S(2)}, u32[]{:S(2)}) %collective-permute-start.2) | collective-permute-done | bytes 524320 | tf_op jit(solution)/shard_map/while/body/eval_jaxpr/ppermute | solution.py:13
  698.6 3.9 collective-permute-done.3
  710.7 3.8 multiply_convert_fusion.2
  721.5 23.9 %collective-permute-done.2 = bf16[256,1024]{0,1:T(8,128)(2,1)} collective-permute-done((bf16[256,1024]{0,1:T(8,128)(2,1)}, bf16[256,1024]{0,1:T(8,128)(2,1)}, u32[]{:S(2)}, u32[]{:S(2)}) %collective-permute-start.2) | collective-permute-done | bytes 524320 | tf_op jit(solution)/shard_map/while/body/eval_jaxpr/ppermute | solution.py:13
  747.5 3.5 collective-permute-done.3
  759.2 3.8 multiply_convert_fusion.2
  770.1 22.9 %collective-permute-done.2 = bf16[256,1024]{0,1:T(8,128)(2,1)} collective-permute-done((bf16[256,1024]{0,1:T(8,128)(2,1)}, bf16[256,1024]{0,1:T(8,128)(2,1)}, u32[]{:S(2)}, u32[]{:S(2)}) %collective-permute-start.2) | collective-permute-done | bytes 524320 | tf_op jit(solution)/shard_map/while/body/eval_jaxpr/ppermute | solution.py:13
  795.1 3.5 collective-permute-done.3
  800.8 3.5 convert_bitcast_fusion.2
  808.7 3.6 convolution_convert_fusion.2
  812.4 7.3 convolution_convert_fusion.1
  821.0 7.2 convolution_convert_fusion
  829.9 10.6 all-reduce.1
  847.3 19.4 %reduce-scatter.9.cloned.1.call-done = bf16[256,1024]{0,1:T(8,128)(2,1)} async-done(((bf16[1024,1024]{0,1:T(8,128)(2,1)}), bf16[256,1024]{0,1:T(8,128)(2,1)}) %reduce-scatter.9.cloned.1.call-update) | async-done | bytes 524304 | tf_op jit(solution)/shard_map/reduce_scatter | solution.py:108
  866.7 34.0 %reduce-scatter.11.cloned.1.call-done = bf16[256,1024]{0,1:T(8,128)(2,1)} async-done(((bf16[1024,1024]{0,1:T(8,128)(2,1)}), bf16[256,1024]{0,1:T(8,128)(2,1)}) %reduce-scatter.11.cloned.1.call-update) | async-done | bytes 524304 | tf_op jit(solution)/shard_map/reduce_scatter | solution.py:108
  900.7 34.0 %reduce-scatter.13.cloned.1.call-done = bf16[256,1024]{1,0:T(8,128)(2,1)} async-done(((bf16[1024,1024]{1,0:T(8,128)(2,1)}), bf16[256,1024]{1,0:T(8,128)(2,1)}) %reduce-scatter.13.cloned.1.call-update) | async-done | bytes 524304 | tf_op jit(solution)/shard_map/reduce_scatter | solution.py:108
  934.7 74.3 %reduce-scatter.15.cloned.1.call-done = bf16[256,4096]{1,0:T(8,128)(2,1)} async-done(((bf16[1024,4096]{1,0:T(8,128)(2,1)}), bf16[256,4096]{1,0:T(8,128)(2,1)}) %reduce-scatter.15.cloned.1.call-update) | async-done | bytes 2097168 | tf_op jit(solution)/shard_map/reduce_scatter | solution.py:108
  1009.0 74.3 %reduce-scatter.17.cloned.1.call-done = bf16[1024,1024]{1,0:T(8,128)(2,1)} async-done(((bf16[4096,1024]{1,0:T(8,128)(2,1)}), bf16[1024,1024]{1,0:T(8,128)(2,1)}) %reduce-scatter.17.cloned.1.call-update) | async-done | bytes 2097168 | tf_op jit(solution)/shard_map/reduce_scatter | solution.py:108
  1083.3 487.6 %all-reduce.3 = (f32[256,1024]{0,1:T(8,128)S(1)}, f32[1024]{0:T(1024)}, f32[256,1024]{0,1:T(8,128)S(1)}, f32[256,1024]{0,1:T(8,128)S(1)}, f32[1024]{0:T(1024)}, ...) all-reduce(bf16[256,1024]{0,1:T(8,128)(2,1)} %reduce-scatter.7.clon, ...), channel_id=1, replica_groups=mesh['ctx'=8,'fsdp'=4] {'ctx'}, use_global_device_ids=true, to_apply=%region_18.19 | all-reduce | flops 3158016 | bytes 18972672 | tf_op jit(solution)/shard_map/psum | solution.py:253
  (503 shorter events, 211.3 us)
Async XLA Ops:
  7.2 51.9 %copy-start.13 = (bf16[1,16,16,1024]{3,2,1,0:T(8,128)(2,1)S(1)}, bf16[1,16,16,1024]{3,2,1,0:T(8,128)(2,1)}, u32[]{:S(2)}) copy-start(bf16[1,16,16,1024]{3,2,1,0:T(8,128)(2,1)} %param.23) | copy-start | bytes 1572868
  7.2 51.9 %copy-start.34 = (f32[1024]{0:T(1024)S(1)}, f32[1024]{0:T(1024)}, u32[]{:S(2)}) copy-start(f32[1024]{0:T(1024)} %param.30) | copy-start | bytes 12292
  7.2 27.7 %all-gather.9.cloned.1.call-start = ((), (), s32[]{:S(2)}) async-start(), calls=%async_computation.6 | async-start | bytes 2621440 | tf_op jit(solution)/shard_map/all_gather | solution.py:165
  7.9 51.2 %all-gather.15.cloned.1.call-start = ((), (), s32[]{:S(2)}) async-start(), calls=%async_computation.9 | async-start | bytes 2621440 | tf_op jit(solution)/shard_map/all_gather | solution.py:166
  8.7 74.6 %all-gather.13.cloned.1.call-start = ((), (), s32[]{:S(2)}) async-start(), calls=%async_computation.8 | async-start | bytes 2621440 | tf_op jit(solution)/shard_map/all_gather | solution.py:164
  9.4 149.9 %all-gather.11.cloned.1.call-start = ((), (), s32[]{:S(2)}) async-start(), calls=%async_computation.7 | async-start | bytes 4718592 | tf_op jit(solution)/shard_map/all_gather | solution.py:180
  38.3 195.3 %all-gather.17.cloned.1.call-start = ((), (), s32[]{:S(2)}) async-start(), calls=%async_computation.10 | async-start | bytes 4718592 | tf_op jit(solution)/shard_map/all_gather | solution.py:181
  62.2 257.9 %all-gather.19.cloned.1.call-start = ((), (), s32[]{:S(2)}) async-start(), calls=%async_computation.11 | async-start | bytes 2621440 | tf_op jit(solution)/shard_map/all_gather | solution.py:167
  62.8 260.2 %all-gather.21.cloned.1.call-start = ((), (), s32[]{:S(2)}) async-start(), calls=%async_computation.12 | async-start | bytes 10485760 | tf_op jit(solution)/shard_map/all_gather | solution.py:168
  63.6 312.0 %all-gather.23.cloned.1.call-start = ((), (), s32[]{:S(2)}) async-start(), calls=%async_computation.13 | async-start | bytes 10485760 | tf_op jit(solution)/shard_map/all_gather | solution.py:169
  64.3 783.0 %reduce-scatter.7.cloned.1.call-start = ((), (), s32[]{:S(2)}) async-start(), calls=%async_computation.14 | async-start | bytes 2621440 | tf_op jit(solution)/shard_map/reduce_scatter | solution.py:108
  233.5 86.6 %copy-start.30 = (f32[1024]{0:T(1024)S(1)}, f32[1024]{0:T(1024)}, u32[]{:S(2)}) copy-start(f32[1024]{0:T(1024)} %param.32) | copy-start | bytes 12292
  322.7 68.7 %copy-start.9 = (f32[256,1024]{1,0:T(8,128)}, f32[256,1024]{1,0:T(8,128)S(1)}, u32[]{:S(2)}) copy-start(f32[256,1024]{1,0:T(8,128)S(1)} %get-tuple-element.767) | copy-start | bytes 3145732
  323.0 52.6 %copy-start.36 = (f32[1024]{0:T(1024)S(1)}, f32[1024]{0:T(1024)}, u32[]{:S(2)}) copy-start(f32[1024]{0:T(1024)} %param.38) | copy-start | bytes 12292
  395.4 52.7 %collective-permute-start = (bf16[256,1024]{0,1:T(8,128)(2,1)S(1)}, bf16[256,1024]{0,1:T(8,128)(2,1)}, u32[]{:S(2)}, u32[]{:S(2)}) collective-permute-start(bf16[256,1024]{0,1:T(8,128)(2,1)S(1)} %copy.106), channel_id=1, source_target_pairs={{28,0},{0,4},{4,8},{8,12},{12,16},{16,20},{20,24},{24,28},{29,1},{... | collective-permute-start | bytes 1572872 | tf_op jit(solution)/shard_map/while/body/eval_jaxpr/ppermute | solution.py:13
  398.7 49.3 %collective-permute-start.1 = (bf16[256,1024]{0,1:T(8,128)(2,1)}, bf16[256,1024]{0,1:T(8,128)(2,1)}, u32[]{:S(2)}, u32[]{:S(2)}) collective-permute-start(bf16[256,1024]{0,1:T(8,128)(2,1)} %copy.107), channel_id=1, source_target_pairs={{28,0},{0,4},{4,8},{8,12},{12,16},{16,20},{20,24},{24,28},{29,1},{... | collective-permute-start | bytes 1572872 | tf_op jit(solution)/shard_map/while/body/eval_jaxpr/ppermute | solution.py:13
  408.5 26.9 %collective-permute-start.2 = (bf16[256,1024]{0,1:T(8,128)(2,1)}, bf16[256,1024]{0,1:T(8,128)(2,1)}, u32[]{:S(2)}, u32[]{:S(2)}) collective-permute-start(bf16[256,1024]{0,1:T(8,128)(2,1)} %fusion.169), channel_id=1, source_target_pairs={{28,0},{0,4},{4,8},{8,12},{12,16},{16,20},{20,24},{24,28},{29,1},{... | collective-permute-start | bytes 1572872 | tf_op jit(solution)/shard_map/while/body/eval_jaxpr/ppermute | solution.py:13
  413.2 32.8 %collective-permute-start.3 = (bf16[256,1024]{0,1:T(8,128)(2,1)}, bf16[256,1024]{0,1:T(8,128)(2,1)}, u32[]{:S(2)}, u32[]{:S(2)}) collective-permute-start(bf16[256,1024]{0,1:T(8,128)(2,1)} %fusion.171), channel_id=1, source_target_pairs={{28,0},{0,4},{4,8},{8,12},{12,16},{16,20},{20,24},{24,28},{29,1},{... | collective-permute-start | bytes 1572872 | tf_op jit(solution)/shard_map/while/body/eval_jaxpr/ppermute | solution.py:13
  415.4 32.6 %copy-start.24 = (bf16[256,1024]{0,1:T(8,128)(2,1)S(1)}, bf16[256,1024]{0,1:T(8,128)(2,1)}, u32[]{:S(2)}) copy-start(bf16[256,1024]{0,1:T(8,128)(2,1)} %copy-done.23) | copy-start | bytes 1572868 | tf_op jit(solution)/shard_map/while
  416.1 32.0 %copy-start.5 = (f32[256,1024]{0,1:T(8,128)}, f32[256,1024]{0,1:T(8,128)S(1)}, u32[]{:S(2)}) copy-start(f32[256,1024]{0,1:T(8,128)S(1)} %bitcast_add_fusion.4) | copy-start | bytes 3145732 | tf_op jit(solution)/shard_map/while
  449.3 51.9 %collective-permute-start = (bf16[256,1024]{0,1:T(8,128)(2,1)S(1)}, bf16[256,1024]{0,1:T(8,128)(2,1)}, u32[]{:S(2)}, u32[]{:S(2)}) collective-permute-start(bf16[256,1024]{0,1:T(8,128)(2,1)S(1)} %copy.106), channel_id=1, source_target_pairs={{28,0},{0,4},{4,8},{8,12},{12,16},{16,20},{20,24},{24,28},{29,1},{... | collective-permute-start | bytes 1572872 | tf_op jit(solution)/shard_map/while/body/eval_jaxpr/ppermute | solution.py:13
  451.2 50.0 %collective-permute-start.1 = (bf16[256,1024]{0,1:T(8,128)(2,1)}, bf16[256,1024]{0,1:T(8,128)(2,1)}, u32[]{:S(2)}, u32[]{:S(2)}) collective-permute-start(bf16[256,1024]{0,1:T(8,128)(2,1)} %copy.107), channel_id=1, source_target_pairs={{28,0},{0,4},{4,8},{8,12},{12,16},{16,20},{20,24},{24,28},{29,1},{... | collective-permute-start | bytes 1572872 | tf_op jit(solution)/shard_map/while/body/eval_jaxpr/ppermute | solution.py:13
  460.6 28.8 %collective-permute-start.2 = (bf16[256,1024]{0,1:T(8,128)(2,1)}, bf16[256,1024]{0,1:T(8,128)(2,1)}, u32[]{:S(2)}, u32[]{:S(2)}) collective-permute-start(bf16[256,1024]{0,1:T(8,128)(2,1)} %fusion.169), channel_id=1, source_target_pairs={{28,0},{0,4},{4,8},{8,12},{12,16},{16,20},{20,24},{24,28},{29,1},{... | collective-permute-start | bytes 1572872 | tf_op jit(solution)/shard_map/while/body/eval_jaxpr/ppermute | solution.py:13
  464.7 34.4 %collective-permute-start.3 = (bf16[256,1024]{0,1:T(8,128)(2,1)}, bf16[256,1024]{0,1:T(8,128)(2,1)}, u32[]{:S(2)}, u32[]{:S(2)}) collective-permute-start(bf16[256,1024]{0,1:T(8,128)(2,1)} %fusion.171), channel_id=1, source_target_pairs={{28,0},{0,4},{4,8},{8,12},{12,16},{16,20},{20,24},{24,28},{29,1},{... | collective-permute-start | bytes 1572872 | tf_op jit(solution)/shard_map/while/body/eval_jaxpr/ppermute | solution.py:13
  467.6 33.6 %copy-start.24 = (bf16[256,1024]{0,1:T(8,128)(2,1)S(1)}, bf16[256,1024]{0,1:T(8,128)(2,1)}, u32[]{:S(2)}) copy-start(bf16[256,1024]{0,1:T(8,128)(2,1)} %copy-done.23) | copy-start | bytes 1572868 | tf_op jit(solution)/shard_map/while
  468.2 33.0 %copy-start.5 = (f32[256,1024]{0,1:T(8,128)}, f32[256,1024]{0,1:T(8,128)S(1)}, u32[]{:S(2)}) copy-start(f32[256,1024]{0,1:T(8,128)S(1)} %bitcast_add_fusion.4) | copy-start | bytes 3145732 | tf_op jit(solution)/shard_map/while
  502.5 51.0 %collective-permute-start = (bf16[256,1024]{0,1:T(8,128)(2,1)S(1)}, bf16[256,1024]{0,1:T(8,128)(2,1)}, u32[]{:S(2)}, u32[]{:S(2)}) collective-permute-start(bf16[256,1024]{0,1:T(8,128)(2,1)S(1)} %copy.106), channel_id=1, source_target_pairs={{28,0},{0,4},{4,8},{8,12},{12,16},{16,20},{20,24},{24,28},{29,1},{... | collective-permute-start | bytes 1572872 | tf_op jit(solution)/shard_map/while/body/eval_jaxpr/ppermute | solution.py:13
  504.3 49.1 %collective-permute-start.1 = (bf16[256,1024]{0,1:T(8,128)(2,1)}, bf16[256,1024]{0,1:T(8,128)(2,1)}, u32[]{:S(2)}, u32[]{:S(2)}) collective-permute-start(bf16[256,1024]{0,1:T(8,128)(2,1)} %copy.107), channel_id=1, source_target_pairs={{28,0},{0,4},{4,8},{8,12},{12,16},{16,20},{20,24},{24,28},{29,1},{... | collective-permute-start | bytes 1572872 | tf_op jit(solution)/shard_map/while/body/eval_jaxpr/ppermute | solution.py:13
  512.6 30.0 %collective-permute-start.2 = (bf16[256,1024]{0,1:T(8,128)(2,1)}, bf16[256,1024]{0,1:T(8,128)(2,1)}, u32[]{:S(2)}, u32[]{:S(2)}) collective-permute-start(bf16[256,1024]{0,1:T(8,128)(2,1)} %fusion.169), channel_id=1, source_target_pairs={{28,0},{0,4},{4,8},{8,12},{12,16},{16,20},{20,24},{24,28},{29,1},{... | collective-permute-start | bytes 1572872 | tf_op jit(solution)/shard_map/while/body/eval_jaxpr/ppermute | solution.py:13
  516.7 34.6 %collective-permute-start.3 = (bf16[256,1024]{0,1:T(8,128)(2,1)}, bf16[256,1024]{0,1:T(8,128)(2,1)}, u32[]{:S(2)}, u32[]{:S(2)}) collective-permute-start(bf16[256,1024]{0,1:T(8,128)(2,1)} %fusion.171), channel_id=1, source_target_pairs={{28,0},{0,4},{4,8},{8,12},{12,16},{16,20},{20,24},{24,28},{29,1},{... | collective-permute-start | bytes 1572872 | tf_op jit(solution)/shard_map/while/body/eval_jaxpr/ppermute | solution.py:13
  518.9 34.5 %copy-start.24 = (bf16[256,1024]{0,1:T(8,128)(2,1)S(1)}, bf16[256,1024]{0,1:T(8,128)(2,1)}, u32[]{:S(2)}) copy-start(bf16[256,1024]{0,1:T(8,128)(2,1)} %copy-done.23) | copy-start | bytes 1572868 | tf_op jit(solution)/shard_map/while
  519.6 33.8 %copy-start.5 = (f32[256,1024]{0,1:T(8,128)}, f32[256,1024]{0,1:T(8,128)S(1)}, u32[]{:S(2)}) copy-start(f32[256,1024]{0,1:T(8,128)S(1)} %bitcast_add_fusion.4) | copy-start | bytes 3145732 | tf_op jit(solution)/shard_map/while
  554.7 50.0 %collective-permute-start = (bf16[256,1024]{0,1:T(8,128)(2,1)S(1)}, bf16[256,1024]{0,1:T(8,128)(2,1)}, u32[]{:S(2)}, u32[]{:S(2)}) collective-permute-start(bf16[256,1024]{0,1:T(8,128)(2,1)S(1)} %copy.106), channel_id=1, source_target_pairs={{28,0},{0,4},{4,8},{8,12},{12,16},{16,20},{20,24},{24,28},{29,1},{... | collective-permute-start | bytes 1572872 | tf_op jit(solution)/shard_map/while/body/eval_jaxpr/ppermute | solution.py:13
  556.6 48.2 %collective-permute-start.1 = (bf16[256,1024]{0,1:T(8,128)(2,1)}, bf16[256,1024]{0,1:T(8,128)(2,1)}, u32[]{:S(2)}, u32[]{:S(2)}) collective-permute-start(bf16[256,1024]{0,1:T(8,128)(2,1)} %copy.107), channel_id=1, source_target_pairs={{28,0},{0,4},{4,8},{8,12},{12,16},{16,20},{20,24},{24,28},{29,1},{... | collective-permute-start | bytes 1572872 | tf_op jit(solution)/shard_map/while/body/eval_jaxpr/ppermute | solution.py:13
  564.8 30.0 %collective-permute-start.2 = (bf16[256,1024]{0,1:T(8,128)(2,1)}, bf16[256,1024]{0,1:T(8,128)(2,1)}, u32[]{:S(2)}, u32[]{:S(2)}) collective-permute-start(bf16[256,1024]{0,1:T(8,128)(2,1)} %fusion.169), channel_id=1, source_target_pairs={{28,0},{0,4},{4,8},{8,12},{12,16},{16,20},{20,24},{24,28},{29,1},{... | collective-permute-start | bytes 1572872 | tf_op jit(solution)/shard_map/while/body/eval_jaxpr/ppermute | solution.py:13
  569.0 33.7 %collective-permute-start.3 = (bf16[256,1024]{0,1:T(8,128)(2,1)}, bf16[256,1024]{0,1:T(8,128)(2,1)}, u32[]{:S(2)}, u32[]{:S(2)}) collective-permute-start(bf16[256,1024]{0,1:T(8,128)(2,1)} %fusion.171), channel_id=1, source_target_pairs={{28,0},{0,4},{4,8},{8,12},{12,16},{16,20},{20,24},{24,28},{29,1},{... | collective-permute-start | bytes 1572872 | tf_op jit(solution)/shard_map/while/body/eval_jaxpr/ppermute | solution.py:13
  569.7 35.0 %copy-start.24 = (bf16[256,1024]{0,1:T(8,128)(2,1)S(1)}, bf16[256,1024]{0,1:T(8,128)(2,1)}, u32[]{:S(2)}) copy-start(bf16[256,1024]{0,1:T(8,128)(2,1)} %copy-done.23) | copy-start | bytes 1572868 | tf_op jit(solution)/shard_map/while
  570.4 34.3 %copy-start.5 = (f32[256,1024]{0,1:T(8,128)}, f32[256,1024]{0,1:T(8,128)S(1)}, u32[]{:S(2)}) copy-start(f32[256,1024]{0,1:T(8,128)S(1)} %bitcast_add_fusion.4) | copy-start | bytes 3145732 | tf_op jit(solution)/shard_map/while
  606.0 49.1 %collective-permute-start = (bf16[256,1024]{0,1:T(8,128)(2,1)S(1)}, bf16[256,1024]{0,1:T(8,128)(2,1)}, u32[]{:S(2)}, u32[]{:S(2)}) collective-permute-start(bf16[256,1024]{0,1:T(8,128)(2,1)S(1)} %copy.106), channel_id=1, source_target_pairs={{28,0},{0,4},{4,8},{8,12},{12,16},{16,20},{20,24},{24,28},{29,1},{... | collective-permute-start | bytes 1572872 | tf_op jit(solution)/shard_map/while/body/eval_jaxpr/ppermute | solution.py:13
  607.9 47.2 %collective-permute-start.1 = (bf16[256,1024]{0,1:T(8,128)(2,1)}, bf16[256,1024]{0,1:T(8,128)(2,1)}, u32[]{:S(2)}, u32[]{:S(2)}) collective-permute-start(bf16[256,1024]{0,1:T(8,128)(2,1)} %copy.107), channel_id=1, source_target_pairs={{28,0},{0,4},{4,8},{8,12},{12,16},{16,20},{20,24},{24,28},{29,1},{... | collective-permute-start | bytes 1572872 | tf_op jit(solution)/shard_map/while/body/eval_jaxpr/ppermute | solution.py:13
  616.1 30.0 %collective-permute-start.2 = (bf16[256,1024]{0,1:T(8,128)(2,1)}, bf16[256,1024]{0,1:T(8,128)(2,1)}, u32[]{:S(2)}, u32[]{:S(2)}) collective-permute-start(bf16[256,1024]{0,1:T(8,128)(2,1)} %fusion.169), channel_id=1, source_target_pairs={{28,0},{0,4},{4,8},{8,12},{12,16},{16,20},{20,24},{24,28},{29,1},{... | collective-permute-start | bytes 1572872 | tf_op jit(solution)/shard_map/while/body/eval_jaxpr/ppermute | solution.py:13
  620.2 32.8 %collective-permute-start.3 = (bf16[256,1024]{0,1:T(8,128)(2,1)}, bf16[256,1024]{0,1:T(8,128)(2,1)}, u32[]{:S(2)}, u32[]{:S(2)}) collective-permute-start(bf16[256,1024]{0,1:T(8,128)(2,1)} %fusion.171), channel_id=1, source_target_pairs={{28,0},{0,4},{4,8},{8,12},{12,16},{16,20},{20,24},{24,28},{29,1},{... | collective-permute-start | bytes 1572872 | tf_op jit(solution)/shard_map/while/body/eval_jaxpr/ppermute | solution.py:13
  621.0 34.1 %copy-start.24 = (bf16[256,1024]{0,1:T(8,128)(2,1)S(1)}, bf16[256,1024]{0,1:T(8,128)(2,1)}, u32[]{:S(2)}) copy-start(bf16[256,1024]{0,1:T(8,128)(2,1)} %copy-done.23) | copy-start | bytes 1572868 | tf_op jit(solution)/shard_map/while
  621.7 33.4 %copy-start.5 = (f32[256,1024]{0,1:T(8,128)}, f32[256,1024]{0,1:T(8,128)S(1)}, u32[]{:S(2)}) copy-start(f32[256,1024]{0,1:T(8,128)S(1)} %bitcast_add_fusion.4) | copy-start | bytes 3145732 | tf_op jit(solution)/shard_map/while
  656.4 48.2 %collective-permute-start = (bf16[256,1024]{0,1:T(8,128)(2,1)S(1)}, bf16[256,1024]{0,1:T(8,128)(2,1)}, u32[]{:S(2)}, u32[]{:S(2)}) collective-permute-start(bf16[256,1024]{0,1:T(8,128)(2,1)S(1)} %copy.106), channel_id=1, source_target_pairs={{28,0},{0,4},{4,8},{8,12},{12,16},{16,20},{20,24},{24,28},{29,1},{... | collective-permute-start | bytes 1572872 | tf_op jit(solution)/shard_map/while/body/eval_jaxpr/ppermute | solution.py:13
  658.2 46.3 %collective-permute-start.1 = (bf16[256,1024]{0,1:T(8,128)(2,1)}, bf16[256,1024]{0,1:T(8,128)(2,1)}, u32[]{:S(2)}, u32[]{:S(2)}) collective-permute-start(bf16[256,1024]{0,1:T(8,128)(2,1)} %copy.107), channel_id=1, source_target_pairs={{28,0},{0,4},{4,8},{8,12},{12,16},{16,20},{20,24},{24,28},{29,1},{... | collective-permute-start | bytes 1572872 | tf_op jit(solution)/shard_map/while/body/eval_jaxpr/ppermute | solution.py:13
  666.5 30.0 %collective-permute-start.2 = (bf16[256,1024]{0,1:T(8,128)(2,1)}, bf16[256,1024]{0,1:T(8,128)(2,1)}, u32[]{:S(2)}, u32[]{:S(2)}) collective-permute-start(bf16[256,1024]{0,1:T(8,128)(2,1)} %fusion.169), channel_id=1, source_target_pairs={{28,0},{0,4},{4,8},{8,12},{12,16},{16,20},{20,24},{24,28},{29,1},{... | collective-permute-start | bytes 1572872 | tf_op jit(solution)/shard_map/while/body/eval_jaxpr/ppermute | solution.py:13
  670.6 31.8 %collective-permute-start.3 = (bf16[256,1024]{0,1:T(8,128)(2,1)}, bf16[256,1024]{0,1:T(8,128)(2,1)}, u32[]{:S(2)}, u32[]{:S(2)}) collective-permute-start(bf16[256,1024]{0,1:T(8,128)(2,1)} %fusion.171), channel_id=1, source_target_pairs={{28,0},{0,4},{4,8},{8,12},{12,16},{16,20},{20,24},{24,28},{29,1},{... | collective-permute-start | bytes 1572872 | tf_op jit(solution)/shard_map/while/body/eval_jaxpr/ppermute | solution.py:13
  671.4 33.2 %copy-start.24 = (bf16[256,1024]{0,1:T(8,128)(2,1)S(1)}, bf16[256,1024]{0,1:T(8,128)(2,1)}, u32[]{:S(2)}) copy-start(bf16[256,1024]{0,1:T(8,128)(2,1)} %copy-done.23) | copy-start | bytes 1572868 | tf_op jit(solution)/shard_map/while
  672.1 32.5 %copy-start.5 = (f32[256,1024]{0,1:T(8,128)}, f32[256,1024]{0,1:T(8,128)S(1)}, u32[]{:S(2)}) copy-start(f32[256,1024]{0,1:T(8,128)S(1)} %bitcast_add_fusion.4) | copy-start | bytes 3145732 | tf_op jit(solution)/shard_map/while
  705.8 47.3 %collective-permute-start = (bf16[256,1024]{0,1:T(8,128)(2,1)S(1)}, bf16[256,1024]{0,1:T(8,128)(2,1)}, u32[]{:S(2)}, u32[]{:S(2)}) collective-permute-start(bf16[256,1024]{0,1:T(8,128)(2,1)S(1)} %copy.106), channel_id=1, source_target_pairs={{28,0},{0,4},{4,8},{8,12},{12,16},{16,20},{20,24},{24,28},{29,1},{... | collective-permute-start | bytes 1572872 | tf_op jit(solution)/shard_map/while/body/eval_jaxpr/ppermute | solution.py:13
  707.7 45.4 %collective-permute-start.1 = (bf16[256,1024]{0,1:T(8,128)(2,1)}, bf16[256,1024]{0,1:T(8,128)(2,1)}, u32[]{:S(2)}, u32[]{:S(2)}) collective-permute-start(bf16[256,1024]{0,1:T(8,128)(2,1)} %copy.107), channel_id=1, source_target_pairs={{28,0},{0,4},{4,8},{8,12},{12,16},{16,20},{20,24},{24,28},{29,1},{... | collective-permute-start | bytes 1572872 | tf_op jit(solution)/shard_map/while/body/eval_jaxpr/ppermute | solution.py:13
  716.0 29.4 %collective-permute-start.2 = (bf16[256,1024]{0,1:T(8,128)(2,1)}, bf16[256,1024]{0,1:T(8,128)(2,1)}, u32[]{:S(2)}, u32[]{:S(2)}) collective-permute-start(bf16[256,1024]{0,1:T(8,128)(2,1)} %fusion.169), channel_id=1, source_target_pairs={{28,0},{0,4},{4,8},{8,12},{12,16},{16,20},{20,24},{24,28},{29,1},{... | collective-permute-start | bytes 1572872 | tf_op jit(solution)/shard_map/while/body/eval_jaxpr/ppermute | solution.py:13
  720.1 30.9 %collective-permute-start.3 = (bf16[256,1024]{0,1:T(8,128)(2,1)}, bf16[256,1024]{0,1:T(8,128)(2,1)}, u32[]{:S(2)}, u32[]{:S(2)}) collective-permute-start(bf16[256,1024]{0,1:T(8,128)(2,1)} %fusion.171), channel_id=1, source_target_pairs={{28,0},{0,4},{4,8},{8,12},{12,16},{16,20},{20,24},{24,28},{29,1},{... | collective-permute-start | bytes 1572872 | tf_op jit(solution)/shard_map/while/body/eval_jaxpr/ppermute | solution.py:13
  720.9 32.3 %copy-start.24 = (bf16[256,1024]{0,1:T(8,128)(2,1)S(1)}, bf16[256,1024]{0,1:T(8,128)(2,1)}, u32[]{:S(2)}) copy-start(bf16[256,1024]{0,1:T(8,128)(2,1)} %copy-done.23) | copy-start | bytes 1572868 | tf_op jit(solution)/shard_map/while
  754.4 46.3 %collective-permute-start = (bf16[256,1024]{0,1:T(8,128)(2,1)S(1)}, bf16[256,1024]{0,1:T(8,128)(2,1)}, u32[]{:S(2)}, u32[]{:S(2)}) collective-permute-start(bf16[256,1024]{0,1:T(8,128)(2,1)S(1)} %copy.106), channel_id=1, source_target_pairs={{28,0},{0,4},{4,8},{8,12},{12,16},{16,20},{20,24},{24,28},{29,1},{... | collective-permute-start | bytes 1572872 | tf_op jit(solution)/shard_map/while/body/eval_jaxpr/ppermute | solution.py:13
  756.3 44.5 %collective-permute-start.1 = (bf16[256,1024]{0,1:T(8,128)(2,1)}, bf16[256,1024]{0,1:T(8,128)(2,1)}, u32[]{:S(2)}, u32[]{:S(2)}) collective-permute-start(bf16[256,1024]{0,1:T(8,128)(2,1)} %copy.107), channel_id=1, source_target_pairs={{28,0},{0,4},{4,8},{8,12},{12,16},{16,20},{20,24},{24,28},{29,1},{... | collective-permute-start | bytes 1572872 | tf_op jit(solution)/shard_map/while/body/eval_jaxpr/ppermute | solution.py:13
  764.5 28.5 %collective-permute-start.2 = (bf16[256,1024]{0,1:T(8,128)(2,1)}, bf16[256,1024]{0,1:T(8,128)(2,1)}, u32[]{:S(2)}, u32[]{:S(2)}) collective-permute-start(bf16[256,1024]{0,1:T(8,128)(2,1)} %fusion.169), channel_id=1, source_target_pairs={{28,0},{0,4},{4,8},{8,12},{12,16},{16,20},{20,24},{24,28},{29,1},{... | collective-permute-start | bytes 1572872 | tf_op jit(solution)/shard_map/while/body/eval_jaxpr/ppermute | solution.py:13
  768.6 30.0 %collective-permute-start.3 = (bf16[256,1024]{0,1:T(8,128)(2,1)}, bf16[256,1024]{0,1:T(8,128)(2,1)}, u32[]{:S(2)}, u32[]{:S(2)}) collective-permute-start(bf16[256,1024]{0,1:T(8,128)(2,1)} %fusion.171), channel_id=1, source_target_pairs={{28,0},{0,4},{4,8},{8,12},{12,16},{16,20},{20,24},{24,28},{29,1},{... | collective-permute-start | bytes 1572872 | tf_op jit(solution)/shard_map/while/body/eval_jaxpr/ppermute | solution.py:13
  804.3 62.4 %reduce-scatter.9.cloned.1.call-start = ((), (), s32[]{:S(2)}) async-start(), calls=%async_computation.15 | async-start | bytes 2621440 | tf_op jit(solution)/shard_map/reduce_scatter | solution.py:108
  806.5 94.2 %reduce-scatter.11.cloned.1.call-start = ((), (), s32[]{:S(2)}) async-start(), calls=%async_computation.16 | async-start | bytes 2621440 | tf_op jit(solution)/shard_map/reduce_scatter | solution.py:108
  808.6 126.1 %reduce-scatter.13.cloned.1.call-start = ((), (), s32[]{:S(2)}) async-start(), calls=%async_computation.17 | async-start | bytes 2621440 | tf_op jit(solution)/shard_map/reduce_scatter | solution.py:108
  812.3 196.7 %reduce-scatter.15.cloned.1.call-start = ((), (), s32[]{:S(2)}) async-start(), calls=%async_computation.18 | async-start | bytes 10485760 | tf_op jit(solution)/shard_map/reduce_scatter | solution.py:108
  819.8 263.6 %reduce-scatter.17.cloned.1.call-start = ((), (), s32[]{:S(2)}) async-start(), calls=%async_computation.19 | async-start | bytes 10485760 | tf_op jit(solution)/shard_map/reduce_scatter | solution.py:108
  (82 other events, 544.5 us)
Sparse Core Ops, SparseCore 0:
  9.6 25.2 all-gather.8
  36.5 22.5 all-gather.14
  60.7 22.5 all-gather.12
  85.8 73.3 all-gather.10
  161.8 71.6 all-gather.16
  234.9 20.8 all-gather.18
  257.4 58.2 all-gather.20
  317.3 58.2 all-gather.22
  804.4 27.9 reduce-scatter.6
  834.9 31.6 reduce-scatter.8
  869.2 31.4 reduce-scatter.10
  903.2 31.4 reduce-scatter.12
  937.3 71.7 reduce-scatter.14
  1011.6 71.6 reduce-scatter.16
